TPU v7x, 256 devices: a whole 4x4x8 slice. The times are simulated.
256 devices in a mesh: grp: 4 (over y), vocab: 32 (over z, x_hi, core), sub: 2 (over x_lo).
Axes of the slice: x: 4 (x_hi: 2, x_lo: 2; x = x_hi * 2 + x_lo), y: 4, z: 8, core: 2. Of those that a mesh axis runs over, the one named last changes fastest.
Arguments:
- teacher_hidden: bfloat16 [512, 16384], P(('vocab', 'sub'), 'grp'), may hold values from -6 to 6
- teacher_head: bfloat16 [16384, 65536], P('grp', ('vocab', 'sub'))
- student_hidden: bfloat16 [512, 8192], P('grp', ('vocab', 'sub')), may hold values from -6 to 6
- student_head: bfloat16 [8192, 65536], P('grp', ('vocab', 'sub'))
- teacher_rest: float32 [512], P('grp'), as said below
- student_rest: float32 [512], P('grp'), as said below
- sampled: int32 [512], replicated, may hold values from 0 to 65535
- assign: int32 [512], replicated, may hold values from 0 to 511, each once
Outputs:
- hidden_grad: bfloat16 [512, 8192], P('grp', ('vocab', 'sub'))
- divergence: float32 [512], P('grp')
- sampled_logprob: float32 [512], P('grp')
Inputs may be any that keep to these rules, and one draw needn't show every extreme that they name: `teacher_rest`: each value exceeds the natural logarithm of 65536 by 2.2 to 6.5. `student_rest`: each value exceeds the natural logarithm of 65536 by 2.2 to 6.5.
All inputs are finite; a program needn't handle non-finite values.
Results may differ from a plain program's by a relative error of at most 0.0049.
Values may be sent and summed in bfloat16 or wider, within the bound.
No kernel may reach another device: no remote copies, remote signals or barrier semaphores. Data moves between devices by JAX's collectives and lax.ppermute only.
A program may use at most 128 MiB of HBM per device.

v0:
```python
import jax
import jax.numpy as jnp
import numpy as np
from jax import lax
from jax.experimental import pallas as pl
from jax.experimental.pallas import tpu as pltpu
from jax.sharding import Mesh, PartitionSpec as P

loss_scale = 256.0
f32, bf16, i16 = jnp.float32, jnp.bfloat16, jnp.int16

AXES = ("y", "zh", "zl", "xh", "c", "xl")
SIZES = (4, 4, 2, 2, 2, 2)
X = ("xh", "xl")
Z = ("zh", "zl")
VOCAB = ("zh", "zl", "xh", "c", "xl")
NY, NX, NZ = 4, 4, 8
TAIL = 16
TOP = 32766.0
VMEM = 40 * 1024 * 1024


def shift(a, axes, n, k):
    return lax.ppermute(a, axes, [(i, (i + k) % n) for i in range(n)])


def other_core(a):
    return lax.ppermute(a, "c", [(0, 1), (1, 0)])


def turn(a, start, n):
    return lax.dynamic_slice_in_dim(jnp.concatenate([a, a], 0), start, n, 0)


def swap_pairs(k):
    return [(s * 4 + t, t * 4 + (s + k) % 4) for s in range(4) for t in range(4)]


def write_coded(part_ref, code_ref, own_ref):
    rows, cols = own_ref.shape
    own_ref[...] = part_ref[:rows, :]
    diagonal = lax.broadcasted_iota(jnp.int32, (rows, rows), 0) == lax.broadcasted_iota(
        jnp.int32, (rows, rows), 1
    )
    for b in range(1, 4):
        part = part_ref[b * rows : (b + 1) * rows, :]
        top = jnp.max(jnp.abs(part), axis=1, keepdims=True)
        power = jnp.ceil(jnp.log(jnp.maximum(top, 1e-30)) * 1.4426950408889634 + 0.001)
        power = jnp.clip(power, -90.0, 126.0)
        code = jnp.floor(part * (jnp.exp(power * -0.6931471805599453) * TOP) + 0.5)
        code = jnp.clip(code, -32767.0, 32767.0)
        code_ref[b - 1, :rows, :] = code.astype(jnp.int32).astype(i16)
        across = jnp.sum(jnp.where(diagonal, power, 0.0), axis=0, keepdims=True)
        across = jnp.broadcast_to(across, (TAIL, rows))
        code_ref[b - 1, rows:, :rows] = across.astype(jnp.int32).astype(i16)
        if cols > rows:
            code_ref[b - 1, rows:, rows:] = jnp.zeros((TAIL, cols - rows), i16)


def in_hbm(n):
    return [pl.BlockSpec(memory_space=pltpu.HBM)] * n


def in_vmem(n):
    return [pl.BlockSpec(memory_space=pltpu.VMEM)] * n


def stay(a):
    return pltpu.with_memory_space_constraint(a, pltpu.HBM)


def keep(a):
    return pltpu.with_memory_space_constraint(a, pltpu.VMEM)


def fetch(pairs, sems):
    copies = [pltpu.make_async_copy(a, b, sems.at[i]) for i, (a, b) in enumerate(pairs)]
    for copy in copies:
        copy.start()
    return copies


def write_product(acc, source, head):
    tile = acc.shape[0] // 2

    @pl.loop(0, 2)
    def _(i):
        rows = pl.ds(pl.multiple_of(i * tile, tile), tile)
        acc[rows, :] = jnp.dot(source[rows, :], head[...], preferred_element_type=f32)


def teacher_kernel(
    ahead_ref, places_ref, mine_ref, other_ref, head_ref, code_ref, own_ref,
    mine, other, head, chosen, acc, mine_sems, other_sems, head_sems,
):
    half, width = mine_ref.shape
    parts = head_sems.shape[0]
    tile = width // parts
    cols = [pl.ds(i * tile, tile) for i in range(parts)]
    got_mine = fetch([(mine_ref.at[:, c], mine.at[:, c]) for c in cols], mine_sems)
    got_other = fetch([(other_ref.at[:, c], other.at[:, c]) for c in cols], other_sems)
    pick = (ahead_ref[...] == places_ref[...]).astype(f32).astype(bf16)
    for i, c in enumerate(cols):
        got_mine[i].wait()
        got_other[i].wait()
        if i == 0:
            got_head = fetch([(head_ref.at[c], head.at[c]) for c in cols], head_sems)
        rows = jnp.dot(pick[:, :half], mine[:, c], preferred_element_type=f32)
        rows += jnp.dot(pick[:, half:], other[:, c], preferred_element_type=f32)
        chosen[:, c] = rows.astype(bf16)
    for copy in got_head:
        copy.wait()
    write_product(acc, chosen, head)
    write_coded(acc, code_ref, own_ref)


def coded_shapes(rows, cols):
    return [
        jax.ShapeDtypeStruct((3, rows + TAIL, cols), i16),
        jax.ShapeDtypeStruct((rows, cols), f32),
    ]


def teacher_part(ahead, places, mine, other, head):
    tokens, (half, width), cols = ahead.shape[0], mine.shape, head.shape[1]
    parts = 4
    return pl.pallas_call(
        teacher_kernel,
        in_specs=in_vmem(2) + in_hbm(3),
        out_specs=in_vmem(2),
        out_shape=coded_shapes(tokens // 4, cols),
        scratch_shapes=[
            pltpu.VMEM((half, width), bf16),
            pltpu.VMEM((half, width), bf16),
            pltpu.VMEM((width, cols), bf16),
            pltpu.VMEM((tokens, width), bf16),
            pltpu.VMEM((tokens, cols), f32),
            pltpu.SemaphoreType.DMA((parts,)),
            pltpu.SemaphoreType.DMA((parts,)),
            pltpu.SemaphoreType.DMA((parts,)),
        ],
        compiler_params=pltpu.CompilerParams(vmem_limit_bytes=VMEM),
        cost_estimate=pl.CostEstimate(
            flops=2 * tokens * width * (cols + tokens),
            bytes_accessed=2 * width * (cols + tokens),
            transcendentals=0,
        ),
        name="teacher_part",
    )(ahead[:, None], places[None, :], stay(mine), stay(other), stay(head))


def student_kernel(
    order_ref, mine_ref, other_ref, head_ref, code_ref, own_ref, hidden, head, acc, head_sems
):
    blocks, _, feats = mine_ref.shape
    parts = head_sems.shape[0]
    tile = head.shape[0] // parts
    spans = [pl.ds(i * tile, tile) for i in range(parts)]
    copies = fetch([(head_ref.at[span], head.at[span]) for span in spans], head_sems)
    for i in range(2 * blocks):
        at = pl.multiple_of(order_ref[i] * feats, feats)
        source = mine_ref if i < blocks else other_ref
        hidden[:, pl.ds(at, feats)] = source[i % blocks]
    for copy in copies:
        copy.wait()
    write_product(acc, hidden, head)
    write_coded(acc, code_ref, own_ref)


def student_part(order, mine, other, head):
    (blocks, tokens, feats), (width, cols) = mine.shape, head.shape
    parts = 4
    return pl.pallas_call(
        student_kernel,
        in_specs=[pl.BlockSpec(memory_space=pltpu.SMEM)] + in_vmem(2) + in_hbm(1),
        out_specs=in_vmem(2),
        out_shape=coded_shapes(tokens // 4, cols),
        scratch_shapes=[
            pltpu.VMEM((tokens, width), bf16),
            pltpu.VMEM((width, cols), bf16),
            pltpu.VMEM((tokens, cols), f32),
            pltpu.SemaphoreType.DMA((parts,)),
        ],
        compiler_params=pltpu.CompilerParams(vmem_limit_bytes=VMEM),
        cost_estimate=pl.CostEstimate(
            flops=2 * tokens * width * cols,
            bytes_accessed=2 * width * (cols + tokens),
            transcendentals=0,
        ),
        name="student_part",
    )(order, mine, other, stay(head))


def gradient_kernel(
    where_ref, own_ref, front_ref, far0_ref, far1_ref, behind_ref, head_ref, out_ref,
    delta,
):
    rows, feats = out_ref.shape[3:]
    half = rows // 2
    core, x, y = where_ref[0], where_ref[1], where_ref[2]

    def put(ahead, start, source):
        at = pl.multiple_of(lax.rem(y + ahead, NY) * rows + start, half)
        delta[pl.ds(at, source.shape[0]), :] = source[...]

    put(0, 0, own_ref)
    put(1, 0, front_ref)
    put(2, 0, far0_ref)
    put(2, half, far1_ref)
    put(3, 0, behind_ref)
    for i in range(4):
        span = pl.ds(pl.multiple_of((2 * i + core) * 2 * feats, 2 * feats), 2 * feats)
        grad = lax.dot_general(
            delta[...], head_ref[span, :], (((1,), (1,)), ((), ())), preferred_element_type=f32
        ).astype(out_ref.dtype)
        for xl in range(2):
            ahead = lax.rem(2 * (i % 2) + xl + NX - x, NX)
            for a in range(4):
                out_ref[ahead, a, i // 2] = grad[
                    a * rows : (a + 1) * rows, xl * feats : (xl + 1) * feats
                ]


def gradient_part(core, x, y, pieces, head, dtype):
    (rows, cols), width = pieces[0].shape, head.shape[0]
    tokens, feats = 4 * rows, width // 16
    return pl.pallas_call(
        gradient_kernel,
        in_specs=[pl.BlockSpec(memory_space=pltpu.SMEM)] + in_vmem(len(pieces) + 1),
        out_specs=in_vmem(1)[0],
        scratch_shapes=[
            pltpu.VMEM((tokens, cols), bf16),
        ],
        out_shape=jax.ShapeDtypeStruct((4, 4, 2, rows, feats), dtype),
        compiler_params=pltpu.CompilerParams(vmem_limit_bytes=VMEM),
        cost_estimate=pl.CostEstimate(
            flops=tokens * width * cols,
            bytes_accessed=width * cols + 2 * tokens * cols,
            transcendentals=0,
        ),
        name="gradient_part",
    )(jnp.stack([core, x, y]).astype(jnp.int32), *pieces, keep(head))


def send_coded(code):
    return [shift(code[k - 1], "y", NY, k) for k in (2, 1, 3)]


def finish_sum(own, received):
    rows = own.shape[0]
    out = own
    for got in received:
        scale = jnp.exp2(got[rows, :rows].astype(f32)) * (1.0 / TOP)
        out = out + got[:rows].astype(f32) * scale[:, None]
    return out


def per_device(
    teacher_hidden,
    teacher_head,
    student_hidden,
    student_head,
    teacher_rest,
    student_rest,
    sampled,
    assign,
):
    y, zh, zl = lax.axis_index("y"), lax.axis_index("zh"), lax.axis_index("zl")
    x, c = lax.axis_index(X), lax.axis_index("c")
    tok_rows, feats = student_hidden.shape
    vocab_cols = student_head.shape[1]
    ahead = lax.dynamic_slice_in_dim(
        jnp.concatenate([assign, assign]), y * tok_rows, 4 * tok_rows, 0
    )
    xs = (x - jnp.arange(NX)) % NX

    n = teacher_hidden.shape[0]
    rows = jnp.concatenate(
        [teacher_hidden] + [shift(teacher_hidden, X, NX, k) for k in range(1, NX)], 0
    )
    rows, student_hidden = lax.optimization_barrier((rows, student_hidden))
    rows = lax.all_gather(rows, Z, axis=0, tiled=True)

    token_ids = jnp.take(sampled, ahead[:tok_rows], axis=0)

    got = jnp.stack(
        [lax.ppermute(student_hidden, ("y", "zh"), swap_pairs(k)) for k in range(4)][::-1]
    )
    got = turn(got, 3 - (zh - y) % 4, 4).reshape(4 * tok_rows, feats)
    got = jnp.stack([got, lax.ppermute(got, "zl", [(0, 1), (1, 0)])])
    got = [got] + [shift(got, X, NX, k) for k in (2, 1, 3)]
    got_other = jnp.concatenate([other_core(g) for g in got], 0)
    got = jnp.concatenate(got, 0)
    xo = (x - jnp.array([0, 2, 1, 3])) % NX
    quarter = jnp.stack([zl, 1 - zl])[None, :] * 8 + (xo // 2 * 4 + xo % 2)[:, None]
    order = (quarter[None] + jnp.stack([c, 1 - c])[:, None, None] * 2).reshape(-1)
    rows, got_other = lax.optimization_barrier((rows, got_other))
    student_code, student_own = student_part(order, got, got_other, student_head)

    student_got = send_coded(student_code)
    rows_other = other_core(rows)
    z_places = jnp.arange(NZ)[:, None] * 8 + (xs // 2 * 4 + xs % 2)[None, :]
    places = jnp.stack([z_places + 2 * c, z_places + 2 * (1 - c)])[..., None] * n + jnp.arange(n)
    teacher_code, teacher_own = teacher_part(
        ahead, places.reshape(-1), rows, rows_other, teacher_head
    )
    student_got, teacher_got = lax.optimization_barrier((student_got, send_coded(teacher_code)))
    student_logit = finish_sum(student_own, student_got)
    teacher_logit = finish_sum(teacher_own, teacher_got)

    col_index = lax.axis_index(VOCAB) * vocab_cols + lax.broadcasted_iota(
        jnp.int32, (1, vocab_cols), 1
    )
    teacher_exp = jnp.exp(teacher_logit - teacher_rest[:, None])
    student_exp = jnp.exp(student_logit - student_rest[:, None])
    sums = jnp.stack(
        [
            jnp.sum(teacher_exp, axis=1),
            jnp.sum(student_exp, axis=1),
            jnp.sum(teacher_exp * (teacher_logit - student_logit), axis=1),
            jnp.sum(jnp.where(col_index == token_ids[:, None], student_logit, 0.0), axis=1),
        ]
    )
    sums = lax.all_to_all(jnp.broadcast_to(sums[None], (64,) + sums.shape), VOCAB, 0, 0)
    teacher_total, student_total, gap, picked = jnp.sum(sums, axis=0)
    teacher_norm = teacher_rest + jnp.log(1.0 + teacher_total)
    student_norm = student_rest + jnp.log(1.0 + student_total)
    teacher_scale = 1.0 / (1.0 + teacher_total)
    student_scale = 1.0 / (1.0 + student_total)
    divergence = (gap - (teacher_norm - student_norm) * teacher_total) * teacher_scale
    sampled_logprob = picked - student_norm

    delta = (
        loss_scale * (student_exp * student_scale[:, None] - teacher_exp * teacher_scale[:, None])
    ).astype(bf16)
    half = tok_rows // 2
    behind = shift(delta, "y", NY, 1)
    front = shift(delta, "y", NY, -1)
    far = [shift(behind[:half], "y", NY, 1), shift(front[half:], "y", NY, -1)]
    pieces = [delta, front] + far + [behind]

    theirs = other_core(gradient_part(1 - c, x, y, pieces, student_head, bf16))
    mine = gradient_part(c, x, y, pieces, student_head, f32)
    both = mine + theirs.astype(f32)
    grad = both[0]
    for k in (2, 1, 3):
        grad = grad + shift(both[k].astype(bf16), X, NX, k).astype(f32)
    grad = lax.all_to_all(grad.astype(bf16).reshape(NZ, tok_rows, feats), Z, 0, 0)
    grad = jnp.sum(grad.astype(f32), axis=0).astype(bf16)
    hidden_grad = lax.ppermute(grad, ("y", "zh"), swap_pairs(0))
    return (hidden_grad, divergence, sampled_logprob)


def solution(mesh):
    fine = Mesh(np.asarray(mesh.devices).reshape(SIZES), AXES)
    return jax.shard_map(
        per_device,
        mesh=fine,
        in_specs=(
            P(VOCAB, "y"),
            P("y", VOCAB),
            P("y", VOCAB),
            P("y", VOCAB),
            P("y"),
            P("y"),
            P(),
            P(),
        ),
        out_specs=(P("y", VOCAB), P("y"), P("y")),
        check_vma=False,
    )
```

profile of v0, /device:TPU:24, one launch (start us, length us, event | category | flops | bytes accessed | tf_op | source)
XLA Modules:
  0.0 198.4 jit_solution(15092099322332494826)
XLA Ops:
  7.2 3.1 %collective-permute-start.1 = (bf16[8,4096]{1,0:T(8,128)(2,1)}, bf16[8,4096]{1,0:T(8,128)(2,1)S(1)}, u32[]{:S(2)}, u32[]{:S(2)}) collective-permute-start(bf16[8,4096]{1,0:T(8,128)(2,1)} %param.9), channel_id=1, source_target_pairs={{0,4},{1,5},{4,0},{5,1},{2,6},{3,7},{6,2},{7,3},{8,12},{9,13},{12,... | collective-permute-start | bytes 196616 | tf_op jit(solution)/shard_map/ppermute | solution.py:24
  17.6 6.9 %collective-permute-start.3 = (bf16[128,128]{1,0:T(8,128)(2,1)}, bf16[128,128]{1,0:T(8,128)(2,1)S(1)}, u32[]{:S(2)}, u32[]{:S(2)}) collective-permute-start(bf16[128,128]{1,0:T(8,128)(2,1)} %param.11), channel_id=1, source_target_pairs={{0,48},{16,112},{32,176},{48,240},{64,0},{80,64},{96,128},{112,192... | collective-permute-start | bytes 98312 | tf_op jit(solution)/shard_map/ppermute | solution.py:287
  24.6 4.0 %collective-permute-start.6 = (bf16[128,128]{1,0:T(8,128)(2,1)}, bf16[128,128]{1,0:T(8,128)(2,1)S(1)}, u32[]{:S(2)}, u32[]{:S(2)}) collective-permute-start(bf16[128,128]{1,0:T(8,128)(2,1)} %param.11), channel_id=1, source_target_pairs={{0,0},{16,64},{32,128},{48,192},{64,16},{80,80},{96,144},{112,208}... | collective-permute-start | bytes 98312 | tf_op jit(solution)/shard_map/ppermute | solution.py:287
  29.1 7.1 %collective-permute-done.4 = bf16[128,128]{1,0:T(8,128)(2,1)S(1)} collective-permute-done((bf16[128,128]{1,0:T(8,128)(2,1)}, bf16[128,128]{1,0:T(8,128)(2,1)S(1)}, u32[]{:S(2)}, u32[]{:S(2)}) %collective-permute-start.4) | collective-permute-done | bytes 32800 | tf_op jit(solution)/shard_map/ppermute | solution.py:287
  38.0 5.0 %collective-permute-done.7 = bf16[512,128]{1,0:T(8,128)(2,1)S(1)} collective-permute-done((bf16[512,128]{1,0:T(8,128)(2,1)S(1)}, bf16[512,128]{1,0:T(8,128)(2,1)S(1)}, u32[]{:S(2)}, u32[]{:S(2)}) %collective-permute-start.7) | collective-permute-done | bytes 131104 | tf_op jit(solution)/shard_map/ppermute | solution.py:290
  43.1 3.0 %collective-permute-start.10 = (bf16[2,512,128]{2,1,0:T(8,128)(2,1)S(1)}, bf16[2,512,128]{2,1,0:T(8,128)(2,1)S(1)}, u32[]{:S(2)}, u32[]{:S(2)}) collective-permute-start(bf16[2,512,128]{2,1,0:T(8,128)(2,1)S(1)} %pad_maximum_fusion.2), channel_id=1, source_target_pairs={{0,5},{1,0},{4,1},{5,4},{2,7},{3,2},{6,3},{7,6},{8,13},{9,8},{12,9... | collective-permute-start | bytes 786440 | tf_op jit(solution)/shard_map/ppermute | solution.py:24
  47.8 6.3 %collective-permute-done.10 = bf16[2,512,128]{2,1,0:T(8,128)(2,1)S(1)} collective-permute-done((bf16[2,512,128]{2,1,0:T(8,128)(2,1)S(1)}, bf16[2,512,128]{2,1,0:T(8,128)(2,1)S(1)}, u32[]{:S(2)}, u32[]{:S(2)}) %collective-permute-start.10) | collective-permute-done | bytes 262176 | tf_op jit(solution)/shard_map/ppermute | solution.py:24
  58.5 5.8 %all-gather.2.cloned.1.call-done.mine_ref = bf16[256,4096]{1,0:T(8,128)(2,1)} async-done(((bf16[32,4096]{1,0:T(8,128)(2,1)}), bf16[256,4096]{1,0:T(8,128)(2,1)}) %all-gather.2.cloned.1.call-update) | async-done | bytes 2097168 | tf_op jit(solution)/shard_map/all_gather | solution.py:282
  66.4 6.4 %student_part.1 = (s16[3,144,1024]{2,1,0:T(8,128)(2,1)S(1)}, f32[128,1024]{1,0:T(8,128)S(1)}) custom-call(s32[16]{0:T(128)S(1)} %add.265.order_ref, bf16[8,512,128]{2,1,0:T(8,128)(2,1)S(1)} %constant_dynamic-update-slice_fusion.mine_ref, bf16[8,512,128]{2,1,0:T(8,128)(2,1)S(1)} %pad_maximum_fusion.other_ref, bf16[2048,1024]{1,0:T(8,128)(2,1)} %head_ref.7), custom_call_target="tpu_custom_call" | custom-call | flops 2147483648 | bytes 6291456 | tf_op jit(solution)/shard_map/student_part/pallas_call | solution.py:173
  72.8 2.7 %collective-permute-start.17 = (s16[144,1024]{1,0:T(8,128)(2,1)S(1)}, s16[144,1024]{1,0:T(8,128)(2,1)S(1)}, u32[]{:S(2)}, u32[]{:S(2)}) collective-permute-start(s16[144,1024]{1,0:T(8,128)(2,1)S(1)} %get-tuple-element.47), channel_id=1, source_target_pairs={{0,192},{64,0},{128,64},{192,128},{1,193},{65,1},{129,65},{193,129... | collective-permute-start | bytes 884744 | tf_op jit(solution)/shard_map/ppermute | solution.py:24
  77.6 10.3 %teacher_part.1 = (s16[3,144,1024]{2,1,0:T(8,128)(2,1)S(1)}, f32[128,1024]{1,0:T(8,128)S(1)}) custom-call(s32[512,1]{1,0:T(8,128)S(1)} %copy.14.ahead_ref, s32[1,512]{1,0:T(1,128)S(1)} %add.282.places_ref, bf16[256,4096]{1,0:T(8,128)(2,1)} %all-gather.2.cloned.1.call-done.mine_ref, bf16[256,4096]{1,0:T(8,128)(2,1)} %collective-permute-done.18.other_ref, ...), custom_call_target="tpu_custom_call" | custom-call | flops 6442450944 | bytes 12582912 | tf_op jit(solution)/shard_map/teacher_part/pallas_call | solution.py:127
  88.1 3.2 %collective-permute-start.20 = (s16[144,1024]{1,0:T(8,128)(2,1)S(1)}, s16[144,1024]{1,0:T(8,128)(2,1)S(1)}, u32[]{:S(2)}, u32[]{:S(2)}) collective-permute-start(s16[144,1024]{1,0:T(8,128)(2,1)S(1)} %get-tuple-element.45), channel_id=1, source_target_pairs={{0,64},{64,128},{128,192},{192,0},{1,65},{65,129},{129,193},{193,1... | collective-permute-start | bytes 884744 | tf_op jit(solution)/shard_map/ppermute | solution.py:24
  92.2 6.9 %collective-permute-done.21 = s16[144,1024]{1,0:T(8,128)(2,1)S(1)} collective-permute-done((s16[144,1024]{1,0:T(8,128)(2,1)S(1)}, s16[144,1024]{1,0:T(8,128)(2,1)S(1)}, u32[]{:S(2)}, u32[]{:S(2)}) %collective-permute-start.21) | collective-permute-done | bytes 294944 | tf_op jit(solution)/shard_map/ppermute | solution.py:24
  99.1 4.6 %collective-permute-done.20 = s16[144,1024]{1,0:T(8,128)(2,1)S(1)} collective-permute-done((s16[144,1024]{1,0:T(8,128)(2,1)S(1)}, s16[144,1024]{1,0:T(8,128)(2,1)S(1)}, u32[]{:S(2)}, u32[]{:S(2)}) %collective-permute-start.20) | collective-permute-done | bytes 294944 | tf_op jit(solution)/shard_map/ppermute | solution.py:24
  106.0 17.2 %all_to_all.10 = f32[64,4,128]{2,1,0:T(4,128)S(1)} all-to-all(f32[64,4,128]{2,1,0:T(4,128)S(1)} %broadcast_in_dim.19), channel_id=1, replica_groups=mesh['y'=4,'zh'=4,'zl'=2,'xh'=2,'c'=2,'xl'=2] {'zh','zl','xh','c','xl'}, dimensions={0} | all-to-all | bytes 262144 | tf_op jit(solution)/shard_map/all_to_all | solution.py:324
  124.0 2.8 %collective-permute-start.23 = (bf16[128,1024]{1,0:T(8,128)(2,1)S(1)}, bf16[128,1024]{1,0:T(8,128)(2,1)S(1)}, u32[]{:S(2)}, u32[]{:S(2)}) collective-permute-start(bf16[128,1024]{1,0:T(8,128)(2,1)S(1)} %multiply_convert_fusion.own_ref), channel_id=1, source_target_pairs={{0,64},{64,128},{128,192},{192,0},{1,65},{65,129},{129,193},{193,1... | collective-permute-start | bytes 786440 | tf_op jit(solution)/shard_map/ppermute | solution.py:24
  126.8 5.9 %collective-permute-done.23.behind_ref = bf16[128,1024]{1,0:T(8,128)(2,1)S(1)} collective-permute-done((bf16[128,1024]{1,0:T(8,128)(2,1)S(1)}, bf16[128,1024]{1,0:T(8,128)(2,1)S(1)}, u32[]{:S(2)}, u32[]{:S(2)}) %collective-permute-start.23) | collective-permute-done | bytes 262176 | tf_op jit(solution)/shard_map/ppermute | solution.py:24
  132.7 3.8 %collective-permute-start.24 = (bf16[64,1024]{1,0:T(8,128)(2,1)S(1)}, bf16[64,1024]{1,0:T(8,128)(2,1)S(1)}, u32[]{:S(2)}, u32[]{:S(2)}) collective-permute-start(bf16[64,1024]{1,0:T(8,128)(2,1)S(1)} %slice.105), channel_id=1, source_target_pairs={{0,64},{64,128},{128,192},{192,0},{1,65},{65,129},{129,193},{193,1... | collective-permute-start | bytes 393224 | tf_op jit(solution)/shard_map/ppermute | solution.py:24
  139.0 3.8 %collective-permute-done.25.far1_ref = bf16[64,1024]{1,0:T(8,128)(2,1)S(1)} collective-permute-done((bf16[64,1024]{1,0:T(8,128)(2,1)S(1)}, bf16[64,1024]{1,0:T(8,128)(2,1)S(1)}, u32[]{:S(2)}, u32[]{:S(2)}) %collective-permute-start.25) | collective-permute-done | bytes 131104 | tf_op jit(solution)/shard_map/ppermute | solution.py:24
  150.5 2.8 %collective-permute-start.29 = (bf16[4,2,128,128]{3,2,1,0:T(8,128)(2,1)S(1)}, bf16[4,2,128,128]{3,2,1,0:T(8,128)(2,1)S(1)}, u32[]{:S(2)}, u32[]{:S(2)}) collective-permute-start(bf16[4,2,128,128]{3,2,1,0:T(8,128)(2,1)S(1)} %get-tuple-element.42), channel_id=1, source_target_pairs={{0,5},{1,0},{4,1},{5,4},{2,7},{3,2},{6,3},{7,6},{8,13},{9,8},{12,9... | collective-permute-start | bytes 786440 | tf_op jit(solution)/shard_map/ppermute | solution.py:24
  153.3 7.5 %collective-permute-done.27 = bf16[4,2,128,128]{3,2,1,0:T(8,128)(2,1)S(1)} collective-permute-done((bf16[4,2,128,128]{3,2,1,0:T(8,128)(2,1)S(1)}, bf16[4,2,128,128]{3,2,1,0:T(8,128)(2,1)S(1)}, u32[]{:S(2)}, u32[]{:S(2)}) %collective-permute-start.27) | collective-permute-done | bytes 262176 | tf_op jit(solution)/shard_map/ppermute | solution.py:24
  160.8 2.7 %collective-permute-done.29 = bf16[4,2,128,128]{3,2,1,0:T(8,128)(2,1)S(1)} collective-permute-done((bf16[4,2,128,128]{3,2,1,0:T(8,128)(2,1)S(1)}, bf16[4,2,128,128]{3,2,1,0:T(8,128)(2,1)S(1)}, u32[]{:S(2)}, u32[]{:S(2)}) %collective-permute-start.29) | collective-permute-done | bytes 262176 | tf_op jit(solution)/shard_map/ppermute | solution.py:24
  165.7 14.7 %all_to_all.11 = bf16[8,128,128]{2,1,0:T(8,128)(2,1)S(1)} all-to-all(bf16[8,128,128]{2,1,0:T(8,128)(2,1)S(1)} %bitcast.97), channel_id=1, replica_groups=mesh['y'=4,'zh'=4,'zl'=2,'xh'=2,'c'=2,'xl'=2] {'zh','zl'}, dimensions={0} | all-to-all | bytes 524288 | tf_op jit(solution)/shard_map/all_to_all | solution.py:348
  182.4 8.4 %collective-permute-done.30 = bf16[128,128]{1,0:T(8,128)(2,1)S(1)} collective-permute-done((bf16[128,128]{1,0:T(8,128)(2,1)S(1)}, bf16[128,128]{1,0:T(8,128)(2,1)S(1)}, u32[]{:S(2)}, u32[]{:S(2)}) %collective-permute-start.30) | collective-permute-done | bytes 32800 | tf_op jit(solution)/shard_map/ppermute | solution.py:350
  (117 shorter events, 39.0 us)
Async XLA Ops:
  7.2 57.2 %all-gather.2.cloned.1.call-start = ((), (), s32[]{:S(2)}) async-start(), calls=%async_computation.2 | async-start | bytes 2359296 | tf_op jit(solution)/shard_map/all_gather | solution.py:282
  7.2 6.4 %collective-permute-start.1 = (bf16[8,4096]{1,0:T(8,128)(2,1)}, bf16[8,4096]{1,0:T(8,128)(2,1)S(1)}, u32[]{:S(2)}, u32[]{:S(2)}) collective-permute-start(bf16[8,4096]{1,0:T(8,128)(2,1)} %param.9), channel_id=1, source_target_pairs={{0,4},{1,5},{4,0},{5,1},{2,6},{3,7},{6,2},{7,3},{8,12},{9,13},{12,... | collective-permute-start | bytes 196616 | tf_op jit(solution)/shard_map/ppermute | solution.py:24
  17.6 11.5 %collective-permute-start.3 = (bf16[128,128]{1,0:T(8,128)(2,1)}, bf16[128,128]{1,0:T(8,128)(2,1)S(1)}, u32[]{:S(2)}, u32[]{:S(2)}) collective-permute-start(bf16[128,128]{1,0:T(8,128)(2,1)} %param.11), channel_id=1, source_target_pairs={{0,48},{16,112},{32,176},{48,240},{64,0},{80,64},{96,128},{112,192... | collective-permute-start | bytes 98312 | tf_op jit(solution)/shard_map/ppermute | solution.py:287
  24.6 11.7 %collective-permute-start.6 = (bf16[128,128]{1,0:T(8,128)(2,1)}, bf16[128,128]{1,0:T(8,128)(2,1)S(1)}, u32[]{:S(2)}, u32[]{:S(2)}) collective-permute-start(bf16[128,128]{1,0:T(8,128)(2,1)} %param.11), channel_id=1, source_target_pairs={{0,0},{16,64},{32,128},{48,192},{64,16},{80,80},{96,144},{112,208}... | collective-permute-start | bytes 98312 | tf_op jit(solution)/shard_map/ppermute | solution.py:287
  28.6 7.7 %collective-permute-start.5 = (bf16[128,128]{1,0:T(8,128)(2,1)}, bf16[128,128]{1,0:T(8,128)(2,1)S(1)}, u32[]{:S(2)}, u32[]{:S(2)}) collective-permute-start(bf16[128,128]{1,0:T(8,128)(2,1)} %param.11), channel_id=1, source_target_pairs={{0,16},{16,80},{32,144},{48,208},{64,32},{80,96},{96,160},{112,224... | collective-permute-start | bytes 98312 | tf_op jit(solution)/shard_map/ppermute | solution.py:287
  28.7 7.6 %collective-permute-start.4 = (bf16[128,128]{1,0:T(8,128)(2,1)}, bf16[128,128]{1,0:T(8,128)(2,1)S(1)}, u32[]{:S(2)}, u32[]{:S(2)}) collective-permute-start(bf16[128,128]{1,0:T(8,128)(2,1)} %param.11), channel_id=1, source_target_pairs={{0,32},{16,96},{32,160},{48,224},{64,48},{80,112},{96,176},{112,24... | collective-permute-start | bytes 98312 | tf_op jit(solution)/shard_map/ppermute | solution.py:287
  36.4 6.6 %collective-permute-start.7 = (bf16[512,128]{1,0:T(8,128)(2,1)S(1)}, bf16[512,128]{1,0:T(8,128)(2,1)S(1)}, u32[]{:S(2)}, u32[]{:S(2)}) collective-permute-start(bf16[512,128]{1,0:T(8,128)(2,1)S(1)} %bitcast.94), channel_id=1, source_target_pairs={{0,8},{8,0},{1,9},{9,1},{2,10},{10,2},{3,11},{11,3},{4,12},{12,4},... | collective-permute-start | bytes 393224 | tf_op jit(solution)/shard_map/ppermute | solution.py:290
  43.1 11.0 %collective-permute-start.10 = (bf16[2,512,128]{2,1,0:T(8,128)(2,1)S(1)}, bf16[2,512,128]{2,1,0:T(8,128)(2,1)S(1)}, u32[]{:S(2)}, u32[]{:S(2)}) collective-permute-start(bf16[2,512,128]{2,1,0:T(8,128)(2,1)S(1)} %pad_maximum_fusion.2), channel_id=1, source_target_pairs={{0,5},{1,0},{4,1},{5,4},{2,7},{3,2},{6,3},{7,6},{8,13},{9,8},{12,9... | collective-permute-start | bytes 786440 | tf_op jit(solution)/shard_map/ppermute | solution.py:24
  46.1 10.4 %collective-permute-start.9 = (bf16[2,512,128]{2,1,0:T(8,128)(2,1)S(1)}, bf16[2,512,128]{2,1,0:T(8,128)(2,1)S(1)}, u32[]{:S(2)}, u32[]{:S(2)}) collective-permute-start(bf16[2,512,128]{2,1,0:T(8,128)(2,1)S(1)} %pad_maximum_fusion.2), channel_id=1, source_target_pairs={{0,1},{1,4},{4,5},{5,0},{2,3},{3,6},{6,7},{7,2},{8,9},{9,12},{12,1... | collective-permute-start | bytes 786440 | tf_op jit(solution)/shard_map/ppermute | solution.py:24
  46.1 10.4 %collective-permute-start.8 = (bf16[2,512,128]{2,1,0:T(8,128)(2,1)S(1)}, bf16[2,512,128]{2,1,0:T(8,128)(2,1)S(1)}, u32[]{:S(2)}, u32[]{:S(2)}) collective-permute-start(bf16[2,512,128]{2,1,0:T(8,128)(2,1)S(1)} %pad_maximum_fusion.2), channel_id=1, source_target_pairs={{0,4},{1,5},{4,0},{5,1},{2,6},{3,7},{6,2},{7,3},{8,12},{9,13},{12,... | collective-permute-start | bytes 786440 | tf_op jit(solution)/shard_map/ppermute | solution.py:24
  47.8 9.4 %collective-permute-start.11 = (bf16[2,512,128]{2,1,0:T(8,128)(2,1)S(1)}, bf16[2,512,128]{2,1,0:T(8,128)(2,1)S(1)}, u32[]{:S(2)}, u32[]{:S(2)}) collective-permute-start(bf16[2,512,128]{2,1,0:T(8,128)(2,1)S(1)} %pad_maximum_fusion.2), channel_id=1, source_target_pairs={{0,2},{2,0},{1,3},{3,1},{4,6},{6,4},{5,7},{7,5},{8,10},{10,8},{9,1... | collective-permute-start | bytes 786440 | tf_op jit(solution)/shard_map/ppermute | solution.py:28
  64.3 13.3 %collective-permute-start.18 = (bf16[256,4096]{1,0:T(8,128)(2,1)}, bf16[256,4096]{1,0:T(8,128)(2,1)}, u32[]{:S(2)}, u32[]{:S(2)}) collective-permute-start(bf16[256,4096]{1,0:T(8,128)(2,1)} %all-gather.2.cloned.1.call-done.mine_ref), channel_id=1, source_target_pairs={{0,2},{2,0},{1,3},{3,1},{4,6},{6,4},{5,7},{7,5},{8,10},{10,8},{9,1... | collective-permute-start | bytes 6291464 | tf_op jit(solution)/shard_map/ppermute | solution.py:28
  72.8 18.6 %collective-permute-start.17 = (s16[144,1024]{1,0:T(8,128)(2,1)S(1)}, s16[144,1024]{1,0:T(8,128)(2,1)S(1)}, u32[]{:S(2)}, u32[]{:S(2)}) collective-permute-start(s16[144,1024]{1,0:T(8,128)(2,1)S(1)} %get-tuple-element.47), channel_id=1, source_target_pairs={{0,192},{64,0},{128,64},{192,128},{1,193},{65,1},{129,65},{193,129... | collective-permute-start | bytes 884744 | tf_op jit(solution)/shard_map/ppermute | solution.py:24
  75.5 16.7 %collective-permute-start.16 = (s16[144,1024]{1,0:T(8,128)(2,1)S(1)}, s16[144,1024]{1,0:T(8,128)(2,1)S(1)}, u32[]{:S(2)}, u32[]{:S(2)}) collective-permute-start(s16[144,1024]{1,0:T(8,128)(2,1)S(1)} %get-tuple-element.48), channel_id=1, source_target_pairs={{0,64},{64,128},{128,192},{192,0},{1,65},{65,129},{129,193},{193,1... | collective-permute-start | bytes 884744 | tf_op jit(solution)/shard_map/ppermute | solution.py:24
  76.1 16.1 %collective-permute-start.15 = (s16[144,1024]{1,0:T(8,128)(2,1)S(1)}, s16[144,1024]{1,0:T(8,128)(2,1)S(1)}, u32[]{:S(2)}, u32[]{:S(2)}) collective-permute-start(s16[144,1024]{1,0:T(8,128)(2,1)S(1)} %get-tuple-element.49), channel_id=1, source_target_pairs={{0,128},{64,192},{128,0},{192,64},{1,129},{65,193},{129,1},{193,65... | collective-permute-start | bytes 884744 | tf_op jit(solution)/shard_map/ppermute | solution.py:24
  88.0 11.0 %collective-permute-start.21 = (s16[144,1024]{1,0:T(8,128)(2,1)S(1)}, s16[144,1024]{1,0:T(8,128)(2,1)S(1)}, u32[]{:S(2)}, u32[]{:S(2)}) collective-permute-start(s16[144,1024]{1,0:T(8,128)(2,1)S(1)} %get-tuple-element.44), channel_id=1, source_target_pairs={{0,192},{64,0},{128,64},{192,128},{1,193},{65,1},{129,65},{193,129... | collective-permute-start | bytes 884744 | tf_op jit(solution)/shard_map/ppermute | solution.py:24
  88.1 15.5 %collective-permute-start.20 = (s16[144,1024]{1,0:T(8,128)(2,1)S(1)}, s16[144,1024]{1,0:T(8,128)(2,1)S(1)}, u32[]{:S(2)}, u32[]{:S(2)}) collective-permute-start(s16[144,1024]{1,0:T(8,128)(2,1)S(1)} %get-tuple-element.45), channel_id=1, source_target_pairs={{0,64},{64,128},{128,192},{192,0},{1,65},{65,129},{129,193},{193,1... | collective-permute-start | bytes 884744 | tf_op jit(solution)/shard_map/ppermute | solution.py:24
  91.4 13.5 %collective-permute-start.19 = (s16[144,1024]{1,0:T(8,128)(2,1)S(1)}, s16[144,1024]{1,0:T(8,128)(2,1)S(1)}, u32[]{:S(2)}, u32[]{:S(2)}) collective-permute-start(s16[144,1024]{1,0:T(8,128)(2,1)S(1)} %get-tuple-element.46), channel_id=1, source_target_pairs={{0,128},{64,192},{128,0},{192,64},{1,129},{65,193},{129,1},{193,65... | collective-permute-start | bytes 884744 | tf_op jit(solution)/shard_map/ppermute | solution.py:24
  124.0 8.6 %collective-permute-start.23 = (bf16[128,1024]{1,0:T(8,128)(2,1)S(1)}, bf16[128,1024]{1,0:T(8,128)(2,1)S(1)}, u32[]{:S(2)}, u32[]{:S(2)}) collective-permute-start(bf16[128,1024]{1,0:T(8,128)(2,1)S(1)} %multiply_convert_fusion.own_ref), channel_id=1, source_target_pairs={{0,64},{64,128},{128,192},{192,0},{1,65},{65,129},{129,193},{193,1... | collective-permute-start | bytes 786440 | tf_op jit(solution)/shard_map/ppermute | solution.py:24
  126.8 9.7 %collective-permute-start.22 = (bf16[128,1024]{1,0:T(8,128)(2,1)S(1)}, bf16[128,1024]{1,0:T(8,128)(2,1)S(1)}, u32[]{:S(2)}, u32[]{:S(2)}) collective-permute-start(bf16[128,1024]{1,0:T(8,128)(2,1)S(1)} %multiply_convert_fusion.own_ref), channel_id=1, source_target_pairs={{0,192},{64,0},{128,64},{192,128},{1,193},{65,1},{129,65},{193,129... | collective-permute-start | bytes 786440 | tf_op jit(solution)/shard_map/ppermute | solution.py:24
  150.0 10.8 %collective-permute-start.27 = (bf16[4,2,128,128]{3,2,1,0:T(8,128)(2,1)S(1)}, bf16[4,2,128,128]{3,2,1,0:T(8,128)(2,1)S(1)}, u32[]{:S(2)}, u32[]{:S(2)}) collective-permute-start(bf16[4,2,128,128]{3,2,1,0:T(8,128)(2,1)S(1)} %get-tuple-element.41), channel_id=1, source_target_pairs={{0,4},{1,5},{4,0},{5,1},{2,6},{3,7},{6,2},{7,3},{8,12},{9,13},{12,... | collective-permute-start | bytes 786440 | tf_op jit(solution)/shard_map/ppermute | solution.py:24
  150.5 13.1 %collective-permute-start.29 = (bf16[4,2,128,128]{3,2,1,0:T(8,128)(2,1)S(1)}, bf16[4,2,128,128]{3,2,1,0:T(8,128)(2,1)S(1)}, u32[]{:S(2)}, u32[]{:S(2)}) collective-permute-start(bf16[4,2,128,128]{3,2,1,0:T(8,128)(2,1)S(1)} %get-tuple-element.42), channel_id=1, source_target_pairs={{0,5},{1,0},{4,1},{5,4},{2,7},{3,2},{6,3},{7,6},{8,13},{9,8},{12,9... | collective-permute-start | bytes 786440 | tf_op jit(solution)/shard_map/ppermute | solution.py:24
  153.3 12.3 %collective-permute-start.28 = (bf16[4,2,128,128]{3,2,1,0:T(8,128)(2,1)S(1)}, bf16[4,2,128,128]{3,2,1,0:T(8,128)(2,1)S(1)}, u32[]{:S(2)}, u32[]{:S(2)}) collective-permute-start(bf16[4,2,128,128]{3,2,1,0:T(8,128)(2,1)S(1)} %get-tuple-element.43), channel_id=1, source_target_pairs={{0,1},{1,4},{4,5},{5,0},{2,3},{3,6},{6,7},{7,2},{8,9},{9,12},{12,1... | collective-permute-start | bytes 786440 | tf_op jit(solution)/shard_map/ppermute | solution.py:24
  180.5 10.4 %collective-permute-start.30 = (bf16[128,128]{1,0:T(8,128)(2,1)S(1)}, bf16[128,128]{1,0:T(8,128)(2,1)S(1)}, u32[]{:S(2)}, u32[]{:S(2)}) collective-permute-start(bf16[128,128]{1,0:T(8,128)(2,1)S(1)} %reduce_sum.62), channel_id=1, source_target_pairs={{0,0},{16,64},{32,128},{48,192},{64,16},{80,80},{96,144},{112,208}... | collective-permute-start | bytes 98312 | tf_op jit(solution)/shard_map/ppermute | solution.py:350
  (13 other events, 207.7 us)
Sparse Core Ops, SparseCore 0:
  17.7 46.5 all-gather.1
where the time goes:
time: 199 us; the launch traced here: 198 us
  waiting for transfers between devices  76.4 us (38%)
  starting transfers between devices  44.6 us (22%)
  blocking collectives  31.9 us (16%)
  Pallas kernels  20.4 us (10%)
  between operations  14.4 us (7%)
  other arithmetic  5.59 us (3%)
  local copies, waits for them, and re-layouts  4.97 us (2%)
    ppermute x19, waiting for transfers between devices, shift(): return lax.ppermute(a, axes, [(i, (i + k) % n) for i in range(n)])  48.1 us
    ppermute x19, starting transfers between devices, shift(): return lax.ppermute(a, axes, [(i, (i + k) % n) for i in range(n)])  29.7 us
    all_to_all x1, blocking collectives, per_device(): lax.all_to_all(jnp.broadcast_to(sums[None], (64,) + sums.shape), VOCAB, 0...  17.2 us
    all_to_all x1, blocking collectives, per_device(): lax.all_to_all(grad.astype(bf16).reshape(NZ, tok_rows, feats), Z, 0, 0)  14.7 us
    ppermute x4, starting transfers between devices, per_device(): lax.ppermute(student_hidden, ('y', 'zh'), swap_pairs(k))  11.5 us
    pallas_call x1, Pallas kernels, teacher_part(): pl.pallas_call(teacher_kernel, in_specs=in_vmem(2) + in_hbm(3), out_specs...  10.3 us
    ppermute x1, waiting for transfers between devices, per_device(): hidden_grad = lax.ppermute(grad, ('y', 'zh'), swap_pairs(0))  8.45 us
    ppermute x4, waiting for transfers between devices, per_device(): lax.ppermute(student_hidden, ('y', 'zh'), swap_pairs(k))  7.12 us
  transfers between devices with their start and end apart: 32, of which 19 were waited for; matrix products, arithmetic and copies ran while one was open for 2% of the time, Pallas kernels for 9%

commit v1 on v0

--- a/solution.py
+++ b/solution.py
@@ -80,37 +80,39 @@
     return copies
 
 
-def write_product(acc, source, head):
-    tile = acc.shape[0] // 2
-
-    @pl.loop(0, 2)
-    def _(i):
-        rows = pl.ds(pl.multiple_of(i * tile, tile), tile)
-        acc[rows, :] = jnp.dot(source[rows, :], head[...], preferred_element_type=f32)
+def add_products(acc, source, head, copies):
+    tile = head.shape[0] // len(copies)
+    for i, copy in enumerate(copies):
+        copy.wait()
+        if i % 2:
+            span = slice((i - 1) * tile, (i + 1) * tile)
+            part = jnp.dot(source[:, span], head[span, :], preferred_element_type=f32)
+            acc[...] = part if i == 1 else acc[...] + part
 
 
 def teacher_kernel(
     ahead_ref, places_ref, mine_ref, other_ref, head_ref, code_ref, own_ref,
-    mine, other, head, chosen, acc, mine_sems, other_sems, head_sems,
+    mine, head, chosen, acc, mine_sems, head_sems,
 ):
     half, width = mine_ref.shape
     parts = head_sems.shape[0]
     tile = width // parts
-    cols = [pl.ds(i * tile, tile) for i in range(parts)]
-    got_mine = fetch([(mine_ref.at[:, c], mine.at[:, c]) for c in cols], mine_sems)
-    got_other = fetch([(other_ref.at[:, c], other.at[:, c]) for c in cols], other_sems)
+    spans = [pl.ds(i * tile, tile) for i in range(parts)]
+    got_mine = fetch([(mine_ref.at[:, span], mine.at[:, span]) for span in spans], mine_sems)
+    copies = fetch([(head_ref.at[span], head.at[span]) for span in spans], head_sems)
     pick = (ahead_ref[...] == places_ref[...]).astype(f32).astype(bf16)
-    for i, c in enumerate(cols):
-        got_mine[i].wait()
-        got_other[i].wait()
-        if i == 0:
-            got_head = fetch([(head_ref.at[c], head.at[c]) for c in cols], head_sems)
-        rows = jnp.dot(pick[:, :half], mine[:, c], preferred_element_type=f32)
-        rows += jnp.dot(pick[:, half:], other[:, c], preferred_element_type=f32)
-        chosen[:, c] = rows.astype(bf16)
-    for copy in got_head:
+
+    for copy in got_mine:
         copy.wait()
-    write_product(acc, chosen, head)
+
+    @pl.loop(0, parts)
+    def _(i):
+        span = pl.ds(pl.multiple_of(i * tile, tile), tile)
+        rows = jnp.dot(pick[:, :half], mine[:, span], preferred_element_type=f32)
+        rows += jnp.dot(pick[:, half:], other_ref[:, span], preferred_element_type=f32)
+        chosen[:, span] = rows.astype(bf16)
+
+    add_products(acc, chosen, head, copies)
     write_coded(acc, code_ref, own_ref)
 
 
@@ -126,16 +128,14 @@
     parts = 4
     return pl.pallas_call(
         teacher_kernel,
-        in_specs=in_vmem(2) + in_hbm(3),
+        in_specs=in_vmem(2) + in_hbm(1) + in_vmem(1) + in_hbm(1),
         out_specs=in_vmem(2),
         out_shape=coded_shapes(tokens // 4, cols),
         scratch_shapes=[
             pltpu.VMEM((half, width), bf16),
-            pltpu.VMEM((half, width), bf16),
             pltpu.VMEM((width, cols), bf16),
             pltpu.VMEM((tokens, width), bf16),
             pltpu.VMEM((tokens, cols), f32),
-            pltpu.SemaphoreType.DMA((parts,)),
             pltpu.SemaphoreType.DMA((parts,)),
             pltpu.SemaphoreType.DMA((parts,)),
         ],
@@ -146,7 +146,7 @@
             transcendentals=0,
         ),
         name="teacher_part",
-    )(ahead[:, None], places[None, :], stay(mine), stay(other), stay(head))
+    )(ahead[:, None], places[None, :], stay(mine), other, stay(head))
 
 
 def student_kernel(
@@ -161,9 +161,7 @@
         at = pl.multiple_of(order_ref[i] * feats, feats)
         source = mine_ref if i < blocks else other_ref
         hidden[:, pl.ds(at, feats)] = source[i % blocks]
-    for copy in copies:
-        copy.wait()
-    write_product(acc, hidden, head)
+    add_products(acc, hidden, head, copies)
     write_coded(acc, code_ref, own_ref)
 
 
@@ -255,6 +253,44 @@
     return out
 
 
+def finish_kernel(got0_ref, got1_ref, got2_ref, own_ref, other_ref, rest_ref, exp_ref, sums_ref):
+    rows = own_ref.shape[0]
+    diagonal = lax.broadcasted_iota(jnp.int32, (rows, rows), 0) == lax.broadcasted_iota(
+        jnp.int32, (rows, rows), 1
+    )
+
+    def upright(line):
+        return jnp.sum(jnp.where(diagonal, line, 0.0), axis=1, keepdims=True)
+
+    def lying(column):
+        return jnp.sum(jnp.where(diagonal, column, 0.0), axis=0, keepdims=True)
+
+    logit = own_ref[...]
+    for got in (got0_ref, got1_ref, got2_ref):
+        power = upright(got[rows:, :rows].astype(jnp.int32).astype(f32)[:1])
+        scale = jnp.exp(power * 0.6931471805599453) * (1.0 / TOP)
+        logit = logit + got[:rows, :].astype(jnp.int32).astype(f32) * scale
+    exps = jnp.exp(logit - upright(rest_ref[...]))
+    exp_ref[...] = exps
+    sums_ref[:1, :] = lying(jnp.sum(exps, axis=1, keepdims=True))
+    sums_ref[1:, :] = lying(jnp.sum(exps * (logit - other_ref[...]), axis=1, keepdims=True))
+
+
+def finish_teacher(got, own, student_logit, rest):
+    rows, cols = own.shape
+    return pl.pallas_call(
+        finish_kernel,
+        in_specs=in_vmem(6),
+        out_specs=in_vmem(2),
+        out_shape=[jax.ShapeDtypeStruct((rows, cols), f32), jax.ShapeDtypeStruct((2, rows), f32)],
+        compiler_params=pltpu.CompilerParams(vmem_limit_bytes=VMEM),
+        cost_estimate=pl.CostEstimate(
+            flops=20 * rows * cols, bytes_accessed=18 * rows * cols, transcendentals=rows * cols
+        ),
+        name="finish_teacher",
+    )(*got, own, student_logit, rest[None, :])
+
+
 def per_device(
     teacher_hidden,
     teacher_head,
@@ -275,28 +311,24 @@
     xs = (x - jnp.arange(NX)) % NX
 
     n = teacher_hidden.shape[0]
-    rows = jnp.concatenate(
-        [teacher_hidden] + [shift(teacher_hidden, X, NX, k) for k in range(1, NX)], 0
-    )
-    rows, student_hidden = lax.optimization_barrier((rows, student_hidden))
+    rows = [teacher_hidden] + [shift(teacher_hidden, X, NX, k) for k in range(1, NX)]
+    mate = lax.ppermute(student_hidden, "zl", [(0, 1), (1, 0)])
+    rows = jnp.concatenate(rows, 0)
+    rows, student_hidden, mate = lax.optimization_barrier((rows, student_hidden, mate))
     rows = lax.all_gather(rows, Z, axis=0, tiled=True)
 
-    token_ids = jnp.take(sampled, ahead[:tok_rows], axis=0)
-
-    got = jnp.stack(
-        [lax.ppermute(student_hidden, ("y", "zh"), swap_pairs(k)) for k in range(4)][::-1]
-    )
-    got = turn(got, 3 - (zh - y) % 4, 4).reshape(4 * tok_rows, feats)
-    got = jnp.stack([got, lax.ppermute(got, "zl", [(0, 1), (1, 0)])])
+    got = jnp.stack([student_hidden, mate])
+    got = jnp.stack([lax.ppermute(got, ("y", "zh"), swap_pairs(k)) for k in range(4)][::-1])
+    got = turn(got, 3 - (zh - y) % 4, 4).transpose(1, 0, 2, 3).reshape(2, 4 * tok_rows, feats)
     got = [got] + [shift(got, X, NX, k) for k in (2, 1, 3)]
     got_other = jnp.concatenate([other_core(g) for g in got], 0)
     got = jnp.concatenate(got, 0)
     xo = (x - jnp.array([0, 2, 1, 3])) % NX
     quarter = jnp.stack([zl, 1 - zl])[None, :] * 8 + (xo // 2 * 4 + xo % 2)[:, None]
     order = (quarter[None] + jnp.stack([c, 1 - c])[:, None, None] * 2).reshape(-1)
-    rows, got_other = lax.optimization_barrier((rows, got_other))
     student_code, student_own = student_part(order, got, got_other, student_head)
 
+    rows, student_code = lax.optimization_barrier((rows, student_code))
     student_got = send_coded(student_code)
     rows_other = other_core(rows)
     z_places = jnp.arange(NZ)[:, None] * 8 + (xs // 2 * 4 + xs % 2)[None, :]
@@ -304,25 +336,29 @@
     teacher_code, teacher_own = teacher_part(
         ahead, places.reshape(-1), rows, rows_other, teacher_head
     )
-    student_got, teacher_got = lax.optimization_barrier((student_got, send_coded(teacher_code)))
+    student_got, teacher_code = lax.optimization_barrier((student_got, teacher_code))
     student_logit = finish_sum(student_own, student_got)
-    teacher_logit = finish_sum(teacher_own, teacher_got)
-
+
+    position = lax.broadcasted_iota(jnp.int32, (1, sampled.shape[0]), 1)
+    token_ids = jnp.sum(
+        jnp.where(ahead[:tok_rows, None] == position, sampled[None, :], 0), axis=1
+    )
     col_index = lax.axis_index(VOCAB) * vocab_cols + lax.broadcasted_iota(
         jnp.int32, (1, vocab_cols), 1
     )
-    teacher_exp = jnp.exp(teacher_logit - teacher_rest[:, None])
     student_exp = jnp.exp(student_logit - student_rest[:, None])
-    sums = jnp.stack(
+    student_sums = jnp.stack(
         [
-            jnp.sum(teacher_exp, axis=1),
             jnp.sum(student_exp, axis=1),
-            jnp.sum(teacher_exp * (teacher_logit - student_logit), axis=1),
             jnp.sum(jnp.where(col_index == token_ids[:, None], student_logit, 0.0), axis=1),
         ]
     )
+    teacher_exp, teacher_sums = finish_teacher(
+        send_coded(teacher_code), teacher_own, student_logit, teacher_rest
+    )
+    sums = jnp.concatenate([teacher_sums, student_sums], 0)
     sums = lax.all_to_all(jnp.broadcast_to(sums[None], (64,) + sums.shape), VOCAB, 0, 0)
-    teacher_total, student_total, gap, picked = jnp.sum(sums, axis=0)
+    teacher_total, gap, student_total, picked = jnp.sum(sums, axis=0)
     teacher_norm = teacher_rest + jnp.log(1.0 + teacher_total)
     student_norm = student_rest + jnp.log(1.0 + student_total)
     teacher_scale = 1.0 / (1.0 + teacher_total)

time: 199 us -> 196 us (0.985)
  waiting for transfers between devices: 76.4 us -> 69 us
  blocking collectives: 31.9 us -> 34.6 us
  Pallas kernels: 20.4 us -> 22.6 us
    ppermute x5, waiting for transfers between devices: 12.1 us -> 8.32 us  [the longest x4 8.21 us: per_device(): lax.ppermute(got, ('y', 'zh'), swap_pairs(k))]
    pallas_call x1 -> x2, Pallas kernels: 10.3 us -> 13.5 us  [the longest x1 12.9 us: teacher_part(): pl.pallas_call(teacher_kernel, in_specs=in_vmem(2) + in_hbm(1) + in_vmem(...]
    ppermute x19, waiting for transfers between devices: 48.1 us -> 45 us  [shift(): return lax.ppermute(a, axes, [(i, (i + k) % n) for i in range(n)])]
    all_to_all x1, blocking collectives: 17.2 us -> 19.8 us  [per_device(): lax.all_to_all(jnp.broadcast_to(sums[None], (64,) + sums.shape), VOCAB, 0...]
  transfers between devices with their start and end apart: 32 -> 32, of which waited for: 19 -> 21; matrix products, arithmetic and copies ran while one was open for 2% -> 3% of each run, Pallas kernels for 9% -> 10%
where the time goes in v1:
time: 196 us; the launch traced here: 195 us
  waiting for transfers between devices  69 us (35%)
  starting transfers between devices  45.1 us (23%)
  blocking collectives  34.6 us (18%)
  Pallas kernels  22.6 us (12%)
  between operations  14.4 us (7%)
  other arithmetic  6.08 us (3%)
  local copies, waits for them, and re-layouts  3.63 us (2%)
    ppermute x19, waiting for transfers between devices, shift(): return lax.ppermute(a, axes, [(i, (i + k) % n) for i in range(n)])  45 us
    ppermute x19, starting transfers between devices, shift(): return lax.ppermute(a, axes, [(i, (i + k) % n) for i in range(n)])  29.2 us
    all_to_all x1, blocking collectives, per_device(): lax.all_to_all(jnp.broadcast_to(sums[None], (64,) + sums.shape), VOCAB, 0...  19.8 us
    all_to_all x1, blocking collectives, per_device(): lax.all_to_all(grad.astype(bf16).reshape(NZ, tok_rows, feats), Z, 0, 0)  14.7 us
    pallas_call x1, Pallas kernels, teacher_part(): pl.pallas_call(teacher_kernel, in_specs=in_vmem(2) + in_hbm(1) + in_vmem(...  12.9 us
    ppermute x4, starting transfers between devices, per_device(): lax.ppermute(got, ('y', 'zh'), swap_pairs(k))  11.4 us
    ppermute x1, waiting for transfers between devices, per_device(): hidden_grad = lax.ppermute(grad, ('y', 'zh'), swap_pairs(0))  8.45 us
    ppermute x4, waiting for transfers between devices, per_device(): lax.ppermute(got, ('y', 'zh'), swap_pairs(k))  8.21 us
  transfers between devices with their start and end apart: 32, of which 21 were waited for; matrix products, arithmetic and copies ran while one was open for 3% of the time, Pallas kernels for 10%

profile of v1, /device:TPU:24, one launch (start us, length us, event | category | flops | bytes accessed | tf_op | source)
XLA Modules:
  0.0 195.4 jit_solution(18170110021834898516)
XLA Ops:
  7.2 3.1 %collective-permute-start.1 = (bf16[8,4096]{1,0:T(8,128)(2,1)}, bf16[8,4096]{1,0:T(8,128)(2,1)S(1)}, u32[]{:S(2)}, u32[]{:S(2)}) collective-permute-start(bf16[8,4096]{1,0:T(8,128)(2,1)} %param.9), channel_id=1, source_target_pairs={{0,4},{1,5},{4,0},{5,1},{2,6},{3,7},{6,2},{7,3},{8,12},{9,13},{12,... | collective-permute-start | bytes 196616 | tf_op jit(solution)/shard_map/ppermute | solution.py:24
  10.9 2.6 %collective-permute-start.2 = (bf16[8,4096]{1,0:T(8,128)(2,1)}, bf16[8,4096]{1,0:T(8,128)(2,1)S(1)}, u32[]{:S(2)}, u32[]{:S(2)}) collective-permute-start(bf16[8,4096]{1,0:T(8,128)(2,1)} %param.9), channel_id=1, source_target_pairs={{0,5},{1,0},{4,1},{5,4},{2,7},{3,2},{6,3},{7,6},{8,13},{9,8},{12,9... | collective-permute-start | bytes 196616 | tf_op jit(solution)/shard_map/ppermute | solution.py:24
  19.2 6.8 %collective-permute-start.4 = (bf16[2,128,128]{2,1,0:T(8,128)(2,1)S(1)}, bf16[2,128,128]{2,1,0:T(8,128)(2,1)S(1)}, u32[]{:S(2)}, u32[]{:S(2)}) collective-permute-start(bf16[2,128,128]{2,1,0:T(8,128)(2,1)S(1)} %pad_maximum_fusion.3), channel_id=1, source_target_pairs={{0,48},{16,112},{32,176},{48,240},{64,0},{80,64},{96,128},{112,192... | collective-permute-start | bytes 196616 | tf_op jit(solution)/shard_map/ppermute | solution.py:321
  26.1 4.0 %collective-permute-start.7 = (bf16[2,128,128]{2,1,0:T(8,128)(2,1)S(1)}, bf16[2,128,128]{2,1,0:T(8,128)(2,1)S(1)}, u32[]{:S(2)}, u32[]{:S(2)}) collective-permute-start(bf16[2,128,128]{2,1,0:T(8,128)(2,1)S(1)} %pad_maximum_fusion.3), channel_id=1, source_target_pairs={{0,0},{16,64},{32,128},{48,192},{64,16},{80,80},{96,144},{112,208}... | collective-permute-start | bytes 196616 | tf_op jit(solution)/shard_map/ppermute | solution.py:321
  30.7 8.2 %collective-permute-done.5 = bf16[2,128,128]{2,1,0:T(8,128)(2,1)S(1)} collective-permute-done((bf16[2,128,128]{2,1,0:T(8,128)(2,1)S(1)}, bf16[2,128,128]{2,1,0:T(8,128)(2,1)S(1)}, u32[]{:S(2)}, u32[]{:S(2)}) %collective-permute-start.5) | collective-permute-done | bytes 65568 | tf_op jit(solution)/shard_map/ppermute | solution.py:321
  39.1 3.6 %collective-permute-start.10 = (bf16[2,512,128]{2,1,0:T(8,128)(2,1)S(1)}, bf16[2,512,128]{2,1,0:T(8,128)(2,1)S(1)}, u32[]{:S(2)}, u32[]{:S(2)}) collective-permute-start(bf16[2,512,128]{2,1,0:T(8,128)(2,1)S(1)} %bitcast.88), channel_id=1, source_target_pairs={{0,5},{1,0},{4,1},{5,4},{2,7},{3,2},{6,3},{7,6},{8,13},{9,8},{12,9... | collective-permute-start | bytes 786440 | tf_op jit(solution)/shard_map/ppermute | solution.py:24
  44.4 2.8 %collective-permute-done.10 = bf16[2,512,128]{2,1,0:T(8,128)(2,1)S(1)} collective-permute-done((bf16[2,512,128]{2,1,0:T(8,128)(2,1)S(1)}, bf16[2,512,128]{2,1,0:T(8,128)(2,1)S(1)}, u32[]{:S(2)}, u32[]{:S(2)}) %collective-permute-start.10) | collective-permute-done | bytes 262176 | tf_op jit(solution)/shard_map/ppermute | solution.py:24
  47.3 5.9 %collective-permute-done.9 = bf16[2,512,128]{2,1,0:T(8,128)(2,1)S(1)} collective-permute-done((bf16[2,512,128]{2,1,0:T(8,128)(2,1)S(1)}, bf16[2,512,128]{2,1,0:T(8,128)(2,1)S(1)}, u32[]{:S(2)}, u32[]{:S(2)}) %collective-permute-start.9) | collective-permute-done | bytes 262176 | tf_op jit(solution)/shard_map/ppermute | solution.py:24
  55.2 5.4 %student_part.1 = (s16[3,144,1024]{2,1,0:T(8,128)(2,1)S(1)}, f32[128,1024]{1,0:T(8,128)S(1)}) custom-call(s32[16]{0:T(128)S(1)} %add.248.order_ref, bf16[8,512,128]{2,1,0:T(8,128)(2,1)S(1)} %pad_maximum_fusion.mine_ref, bf16[8,512,128]{2,1,0:T(8,128)(2,1)S(1)} %pad_maximum_fusion.1.other_ref, bf16[2048,1024]{1,0:T(8,128)(2,1)} %head_ref.7), custom_call_target="tpu_custom_call" | custom-call | flops 2147483648 | bytes 6291456 | tf_op jit(solution)/shard_map/student_part/pallas_call | solution.py:171
  60.6 5.2 %all-gather.2.cloned.1.call-done.mine_ref = bf16[256,4096]{1,0:T(8,128)(2,1)} async-done(((bf16[32,4096]{1,0:T(8,128)(2,1)}), bf16[256,4096]{1,0:T(8,128)(2,1)}) %all-gather.2.cloned.1.call-update) | async-done | bytes 2097168 | tf_op jit(solution)/shard_map/all_gather | solution.py:318
  70.4 12.9 %teacher_part.1 = (s16[3,144,1024]{2,1,0:T(8,128)(2,1)S(1)}, f32[128,1024]{1,0:T(8,128)S(1)}) custom-call(s32[512,1]{1,0:T(8,128)S(1)} %copy.18.ahead_ref, s32[1,512]{1,0:T(1,128)S(1)} %add.265.places_ref, bf16[256,4096]{1,0:T(8,128)(2,1)} %all-gather.2.cloned.1.call-done.mine_ref, bf16[256,4096]{1,0:T(8,128)(2,1)} %collective-permute-done.18.other_ref, ...), custom_call_target="tpu_custom_call" | custom-call | flops 6442450944 | bytes 12582912 | tf_op jit(solution)/shard_map/teacher_part/pallas_call | solution.py:129
  84.8 2.4 %collective-permute-start.20 = (s16[144,1024]{1,0:T(8,128)(2,1)S(1)}, s16[144,1024]{1,0:T(8,128)(2,1)S(1)}, u32[]{:S(2)}, u32[]{:S(2)}) collective-permute-start(s16[144,1024]{1,0:T(8,128)(2,1)S(1)} %get-tuple-element.44), channel_id=1, source_target_pairs={{0,64},{64,128},{128,192},{192,0},{1,65},{65,129},{129,193},{193,1... | collective-permute-start | bytes 884744 | tf_op jit(solution)/shard_map/ppermute | solution.py:24
  89.2 6.9 %collective-permute-done.21.got2_ref = s16[144,1024]{1,0:T(8,128)(2,1)S(1)} collective-permute-done((s16[144,1024]{1,0:T(8,128)(2,1)S(1)}, s16[144,1024]{1,0:T(8,128)(2,1)S(1)}, u32[]{:S(2)}, u32[]{:S(2)}) %collective-permute-start.21) | collective-permute-done | bytes 294944 | tf_op jit(solution)/shard_map/ppermute | solution.py:24
  96.1 3.3 %collective-permute-done.20.got1_ref = s16[144,1024]{1,0:T(8,128)(2,1)S(1)} collective-permute-done((s16[144,1024]{1,0:T(8,128)(2,1)S(1)}, s16[144,1024]{1,0:T(8,128)(2,1)S(1)}, u32[]{:S(2)}, u32[]{:S(2)}) %collective-permute-start.20) | collective-permute-done | bytes 294944 | tf_op jit(solution)/shard_map/ppermute | solution.py:24
  100.8 19.8 %all_to_all.10 = f32[64,4,128]{2,1,0:T(4,128)S(1)} all-to-all(f32[64,4,128]{2,1,0:T(4,128)S(1)} %broadcast_in_dim.27), channel_id=1, replica_groups=mesh['y'=4,'zh'=4,'zl'=2,'xh'=2,'c'=2,'xl'=2] {'zh','zl','xh','c','xl'}, dimensions={0} | all-to-all | bytes 262144 | tf_op jit(solution)/shard_map/all_to_all | solution.py:360
  121.4 2.4 %collective-permute-start.23 = (bf16[128,1024]{1,0:T(8,128)(2,1)S(1)}, bf16[128,1024]{1,0:T(8,128)(2,1)S(1)}, u32[]{:S(2)}, u32[]{:S(2)}) collective-permute-start(bf16[128,1024]{1,0:T(8,128)(2,1)S(1)} %multiply_convert_fusion.own_ref), channel_id=1, source_target_pairs={{0,64},{64,128},{128,192},{192,0},{1,65},{65,129},{129,193},{193,1... | collective-permute-start | bytes 786440 | tf_op jit(solution)/shard_map/ppermute | solution.py:24
  123.8 6.0 %collective-permute-done.23.behind_ref = bf16[128,1024]{1,0:T(8,128)(2,1)S(1)} collective-permute-done((bf16[128,1024]{1,0:T(8,128)(2,1)S(1)}, bf16[128,1024]{1,0:T(8,128)(2,1)S(1)}, u32[]{:S(2)}, u32[]{:S(2)}) %collective-permute-start.23) | collective-permute-done | bytes 262176 | tf_op jit(solution)/shard_map/ppermute | solution.py:24
  129.9 3.6 %collective-permute-start.24 = (bf16[64,1024]{1,0:T(8,128)(2,1)S(1)}, bf16[64,1024]{1,0:T(8,128)(2,1)S(1)}, u32[]{:S(2)}, u32[]{:S(2)}) collective-permute-start(bf16[64,1024]{1,0:T(8,128)(2,1)S(1)} %slice.79), channel_id=1, source_target_pairs={{0,64},{64,128},{128,192},{192,0},{1,65},{65,129},{129,193},{193,1... | collective-permute-start | bytes 393224 | tf_op jit(solution)/shard_map/ppermute | solution.py:24
  136.0 3.8 %collective-permute-done.25.far1_ref = bf16[64,1024]{1,0:T(8,128)(2,1)S(1)} collective-permute-done((bf16[64,1024]{1,0:T(8,128)(2,1)S(1)}, bf16[64,1024]{1,0:T(8,128)(2,1)S(1)}, u32[]{:S(2)}, u32[]{:S(2)}) %collective-permute-start.25) | collective-permute-done | bytes 131104 | tf_op jit(solution)/shard_map/ppermute | solution.py:24
  147.5 2.8 %collective-permute-start.29 = (bf16[4,2,128,128]{3,2,1,0:T(8,128)(2,1)S(1)}, bf16[4,2,128,128]{3,2,1,0:T(8,128)(2,1)S(1)}, u32[]{:S(2)}, u32[]{:S(2)}) collective-permute-start(bf16[4,2,128,128]{3,2,1,0:T(8,128)(2,1)S(1)} %get-tuple-element.41), channel_id=1, source_target_pairs={{0,5},{1,0},{4,1},{5,4},{2,7},{3,2},{6,3},{7,6},{8,13},{9,8},{12,9... | collective-permute-start | bytes 786440 | tf_op jit(solution)/shard_map/ppermute | solution.py:24
  150.3 7.5 %collective-permute-done.27 = bf16[4,2,128,128]{3,2,1,0:T(8,128)(2,1)S(1)} collective-permute-done((bf16[4,2,128,128]{3,2,1,0:T(8,128)(2,1)S(1)}, bf16[4,2,128,128]{3,2,1,0:T(8,128)(2,1)S(1)}, u32[]{:S(2)}, u32[]{:S(2)}) %collective-permute-start.27) | collective-permute-done | bytes 262176 | tf_op jit(solution)/shard_map/ppermute | solution.py:24
  157.8 2.7 %collective-permute-done.29 = bf16[4,2,128,128]{3,2,1,0:T(8,128)(2,1)S(1)} collective-permute-done((bf16[4,2,128,128]{3,2,1,0:T(8,128)(2,1)S(1)}, bf16[4,2,128,128]{3,2,1,0:T(8,128)(2,1)S(1)}, u32[]{:S(2)}, u32[]{:S(2)}) %collective-permute-start.29) | collective-permute-done | bytes 262176 | tf_op jit(solution)/shard_map/ppermute | solution.py:24
  162.7 14.7 %all_to_all.11 = bf16[8,128,128]{2,1,0:T(8,128)(2,1)S(1)} all-to-all(bf16[8,128,128]{2,1,0:T(8,128)(2,1)S(1)} %bitcast.87), channel_id=1, replica_groups=mesh['y'=4,'zh'=4,'zl'=2,'xh'=2,'c'=2,'xl'=2] {'zh','zl'}, dimensions={0} | all-to-all | bytes 524288 | tf_op jit(solution)/shard_map/all_to_all | solution.py:384
  179.4 8.4 %collective-permute-done.30 = bf16[128,128]{1,0:T(8,128)(2,1)S(1)} collective-permute-done((bf16[128,128]{1,0:T(8,128)(2,1)S(1)}, bf16[128,128]{1,0:T(8,128)(2,1)S(1)}, u32[]{:S(2)}, u32[]{:S(2)}) %collective-permute-start.30) | collective-permute-done | bytes 32800 | tf_op jit(solution)/shard_map/ppermute | solution.py:386
  (110 shorter events, 35.9 us)
Async XLA Ops:
  7.2 58.7 %all-gather.2.cloned.1.call-start = ((), (), s32[]{:S(2)}) async-start(), calls=%async_computation.2 | async-start | bytes 2359296 | tf_op jit(solution)/shard_map/all_gather | solution.py:318
  7.2 8.3 %collective-permute-start.1 = (bf16[8,4096]{1,0:T(8,128)(2,1)}, bf16[8,4096]{1,0:T(8,128)(2,1)S(1)}, u32[]{:S(2)}, u32[]{:S(2)}) collective-permute-start(bf16[8,4096]{1,0:T(8,128)(2,1)} %param.9), channel_id=1, source_target_pairs={{0,4},{1,5},{4,0},{5,1},{2,6},{3,7},{6,2},{7,3},{8,12},{9,13},{12,... | collective-permute-start | bytes 196616 | tf_op jit(solution)/shard_map/ppermute | solution.py:24
  19.2 11.5 %collective-permute-start.4 = (bf16[2,128,128]{2,1,0:T(8,128)(2,1)S(1)}, bf16[2,128,128]{2,1,0:T(8,128)(2,1)S(1)}, u32[]{:S(2)}, u32[]{:S(2)}) collective-permute-start(bf16[2,128,128]{2,1,0:T(8,128)(2,1)S(1)} %pad_maximum_fusion.3), channel_id=1, source_target_pairs={{0,48},{16,112},{32,176},{48,240},{64,0},{80,64},{96,128},{112,192... | collective-permute-start | bytes 196616 | tf_op jit(solution)/shard_map/ppermute | solution.py:321
  26.1 12.8 %collective-permute-start.7 = (bf16[2,128,128]{2,1,0:T(8,128)(2,1)S(1)}, bf16[2,128,128]{2,1,0:T(8,128)(2,1)S(1)}, u32[]{:S(2)}, u32[]{:S(2)}) collective-permute-start(bf16[2,128,128]{2,1,0:T(8,128)(2,1)S(1)} %pad_maximum_fusion.3), channel_id=1, source_target_pairs={{0,0},{16,64},{32,128},{48,192},{64,16},{80,80},{96,144},{112,208}... | collective-permute-start | bytes 196616 | tf_op jit(solution)/shard_map/ppermute | solution.py:321
  30.2 8.8 %collective-permute-start.6 = (bf16[2,128,128]{2,1,0:T(8,128)(2,1)S(1)}, bf16[2,128,128]{2,1,0:T(8,128)(2,1)S(1)}, u32[]{:S(2)}, u32[]{:S(2)}) collective-permute-start(bf16[2,128,128]{2,1,0:T(8,128)(2,1)S(1)} %pad_maximum_fusion.3), channel_id=1, source_target_pairs={{0,16},{16,80},{32,144},{48,208},{64,32},{80,96},{96,160},{112,224... | collective-permute-start | bytes 196616 | tf_op jit(solution)/shard_map/ppermute | solution.py:321
  30.2 8.7 %collective-permute-start.5 = (bf16[2,128,128]{2,1,0:T(8,128)(2,1)S(1)}, bf16[2,128,128]{2,1,0:T(8,128)(2,1)S(1)}, u32[]{:S(2)}, u32[]{:S(2)}) collective-permute-start(bf16[2,128,128]{2,1,0:T(8,128)(2,1)S(1)} %pad_maximum_fusion.3), channel_id=1, source_target_pairs={{0,32},{16,96},{32,160},{48,224},{64,48},{80,112},{96,176},{112,24... | collective-permute-start | bytes 196616 | tf_op jit(solution)/shard_map/ppermute | solution.py:321
  39.1 8.1 %collective-permute-start.10 = (bf16[2,512,128]{2,1,0:T(8,128)(2,1)S(1)}, bf16[2,512,128]{2,1,0:T(8,128)(2,1)S(1)}, u32[]{:S(2)}, u32[]{:S(2)}) collective-permute-start(bf16[2,512,128]{2,1,0:T(8,128)(2,1)S(1)} %bitcast.88), channel_id=1, source_target_pairs={{0,5},{1,0},{4,1},{5,4},{2,7},{3,2},{6,3},{7,6},{8,13},{9,8},{12,9... | collective-permute-start | bytes 786440 | tf_op jit(solution)/shard_map/ppermute | solution.py:24
  42.7 10.4 %collective-permute-start.9 = (bf16[2,512,128]{2,1,0:T(8,128)(2,1)S(1)}, bf16[2,512,128]{2,1,0:T(8,128)(2,1)S(1)}, u32[]{:S(2)}, u32[]{:S(2)}) collective-permute-start(bf16[2,512,128]{2,1,0:T(8,128)(2,1)S(1)} %bitcast.89), channel_id=1, source_target_pairs={{0,1},{1,4},{4,5},{5,0},{2,3},{3,6},{6,7},{7,2},{8,9},{9,12},{12,1... | collective-permute-start | bytes 786440 | tf_op jit(solution)/shard_map/ppermute | solution.py:24
  42.7 10.4 %collective-permute-start.8 = (bf16[2,512,128]{2,1,0:T(8,128)(2,1)S(1)}, bf16[2,512,128]{2,1,0:T(8,128)(2,1)S(1)}, u32[]{:S(2)}, u32[]{:S(2)}) collective-permute-start(bf16[2,512,128]{2,1,0:T(8,128)(2,1)S(1)} %bitcast.90), channel_id=1, source_target_pairs={{0,4},{1,5},{4,0},{5,1},{2,6},{3,7},{6,2},{7,3},{8,12},{9,13},{12,... | collective-permute-start | bytes 786440 | tf_op jit(solution)/shard_map/ppermute | solution.py:24
  44.4 9.5 %collective-permute-start.11 = (bf16[2,512,128]{2,1,0:T(8,128)(2,1)S(1)}, bf16[2,512,128]{2,1,0:T(8,128)(2,1)S(1)}, u32[]{:S(2)}, u32[]{:S(2)}) collective-permute-start(bf16[2,512,128]{2,1,0:T(8,128)(2,1)S(1)} %bitcast.91), channel_id=1, source_target_pairs={{0,2},{2,0},{1,3},{3,1},{4,6},{6,4},{5,7},{7,5},{8,10},{10,8},{9,1... | collective-permute-start | bytes 786440 | tf_op jit(solution)/shard_map/ppermute | solution.py:28
  47.3 6.7 %collective-permute-start.14 = (bf16[2,512,128]{2,1,0:T(8,128)(2,1)S(1)}, bf16[2,512,128]{2,1,0:T(8,128)(2,1)S(1)}, u32[]{:S(2)}, u32[]{:S(2)}) collective-permute-start(bf16[2,512,128]{2,1,0:T(8,128)(2,1)S(1)} %collective-permute-done.10), channel_id=1, source_target_pairs={{0,2},{2,0},{1,3},{3,1},{4,6},{6,4},{5,7},{7,5},{8,10},{10,8},{9,1... | collective-permute-start | bytes 786440 | tf_op jit(solution)/shard_map/ppermute | solution.py:28
  66.7 17.0 %collective-permute-start.17 = (s16[144,1024]{1,0:T(8,128)(2,1)S(1)}, s16[144,1024]{1,0:T(8,128)(2,1)S(1)}, u32[]{:S(2)}, u32[]{:S(2)}) collective-permute-start(s16[144,1024]{1,0:T(8,128)(2,1)S(1)} %get-tuple-element.46), channel_id=1, source_target_pairs={{0,192},{64,0},{128,64},{192,128},{1,193},{65,1},{129,65},{193,129... | collective-permute-start | bytes 884744 | tf_op jit(solution)/shard_map/ppermute | solution.py:24
  68.0 15.7 %collective-permute-start.16 = (s16[144,1024]{1,0:T(8,128)(2,1)S(1)}, s16[144,1024]{1,0:T(8,128)(2,1)S(1)}, u32[]{:S(2)}, u32[]{:S(2)}) collective-permute-start(s16[144,1024]{1,0:T(8,128)(2,1)S(1)} %get-tuple-element.47), channel_id=1, source_target_pairs={{0,64},{64,128},{128,192},{192,0},{1,65},{65,129},{129,193},{193,1... | collective-permute-start | bytes 884744 | tf_op jit(solution)/shard_map/ppermute | solution.py:24
  70.0 13.7 %collective-permute-start.15 = (s16[144,1024]{1,0:T(8,128)(2,1)S(1)}, s16[144,1024]{1,0:T(8,128)(2,1)S(1)}, u32[]{:S(2)}, u32[]{:S(2)}) collective-permute-start(s16[144,1024]{1,0:T(8,128)(2,1)S(1)} %get-tuple-element.48), channel_id=1, source_target_pairs={{0,128},{64,192},{128,0},{192,64},{1,129},{65,193},{129,1},{193,65... | collective-permute-start | bytes 884744 | tf_op jit(solution)/shard_map/ppermute | solution.py:24
  83.8 12.3 %collective-permute-start.21 = (s16[144,1024]{1,0:T(8,128)(2,1)S(1)}, s16[144,1024]{1,0:T(8,128)(2,1)S(1)}, u32[]{:S(2)}, u32[]{:S(2)}) collective-permute-start(s16[144,1024]{1,0:T(8,128)(2,1)S(1)} %get-tuple-element.43), channel_id=1, source_target_pairs={{0,192},{64,0},{128,64},{192,128},{1,193},{65,1},{129,65},{193,129... | collective-permute-start | bytes 884744 | tf_op jit(solution)/shard_map/ppermute | solution.py:24
  84.8 14.6 %collective-permute-start.20 = (s16[144,1024]{1,0:T(8,128)(2,1)S(1)}, s16[144,1024]{1,0:T(8,128)(2,1)S(1)}, u32[]{:S(2)}, u32[]{:S(2)}) collective-permute-start(s16[144,1024]{1,0:T(8,128)(2,1)S(1)} %get-tuple-element.44), channel_id=1, source_target_pairs={{0,64},{64,128},{128,192},{192,0},{1,65},{65,129},{129,193},{193,1... | collective-permute-start | bytes 884744 | tf_op jit(solution)/shard_map/ppermute | solution.py:24
  87.1 13.0 %collective-permute-start.19 = (s16[144,1024]{1,0:T(8,128)(2,1)S(1)}, s16[144,1024]{1,0:T(8,128)(2,1)S(1)}, u32[]{:S(2)}, u32[]{:S(2)}) collective-permute-start(s16[144,1024]{1,0:T(8,128)(2,1)S(1)} %get-tuple-element.45), channel_id=1, source_target_pairs={{0,128},{64,192},{128,0},{192,64},{1,129},{65,193},{129,1},{193,65... | collective-permute-start | bytes 884744 | tf_op jit(solution)/shard_map/ppermute | solution.py:24
  121.4 8.4 %collective-permute-start.23 = (bf16[128,1024]{1,0:T(8,128)(2,1)S(1)}, bf16[128,1024]{1,0:T(8,128)(2,1)S(1)}, u32[]{:S(2)}, u32[]{:S(2)}) collective-permute-start(bf16[128,1024]{1,0:T(8,128)(2,1)S(1)} %multiply_convert_fusion.own_ref), channel_id=1, source_target_pairs={{0,64},{64,128},{128,192},{192,0},{1,65},{65,129},{129,193},{193,1... | collective-permute-start | bytes 786440 | tf_op jit(solution)/shard_map/ppermute | solution.py:24
  123.8 9.7 %collective-permute-start.22 = (bf16[128,1024]{1,0:T(8,128)(2,1)S(1)}, bf16[128,1024]{1,0:T(8,128)(2,1)S(1)}, u32[]{:S(2)}, u32[]{:S(2)}) collective-permute-start(bf16[128,1024]{1,0:T(8,128)(2,1)S(1)} %multiply_convert_fusion.own_ref), channel_id=1, source_target_pairs={{0,192},{64,0},{128,64},{192,128},{1,193},{65,1},{129,65},{193,129... | collective-permute-start | bytes 786440 | tf_op jit(solution)/shard_map/ppermute | solution.py:24
  133.5 6.3 %collective-permute-start.25 = (bf16[64,1024]{1,0:T(8,128)(2,1)S(1)}, bf16[64,1024]{1,0:T(8,128)(2,1)S(1)}, u32[]{:S(2)}, u32[]{:S(2)}) collective-permute-start(bf16[64,1024]{1,0:T(8,128)(2,1)S(1)} %slice.80), channel_id=1, source_target_pairs={{0,192},{64,0},{128,64},{192,128},{1,193},{65,1},{129,65},{193,129... | collective-permute-start | bytes 393224 | tf_op jit(solution)/shard_map/ppermute | solution.py:24
  147.0 10.8 %collective-permute-start.27 = (bf16[4,2,128,128]{3,2,1,0:T(8,128)(2,1)S(1)}, bf16[4,2,128,128]{3,2,1,0:T(8,128)(2,1)S(1)}, u32[]{:S(2)}, u32[]{:S(2)}) collective-permute-start(bf16[4,2,128,128]{3,2,1,0:T(8,128)(2,1)S(1)} %get-tuple-element.40), channel_id=1, source_target_pairs={{0,4},{1,5},{4,0},{5,1},{2,6},{3,7},{6,2},{7,3},{8,12},{9,13},{12,... | collective-permute-start | bytes 786440 | tf_op jit(solution)/shard_map/ppermute | solution.py:24
  147.5 13.1 %collective-permute-start.29 = (bf16[4,2,128,128]{3,2,1,0:T(8,128)(2,1)S(1)}, bf16[4,2,128,128]{3,2,1,0:T(8,128)(2,1)S(1)}, u32[]{:S(2)}, u32[]{:S(2)}) collective-permute-start(bf16[4,2,128,128]{3,2,1,0:T(8,128)(2,1)S(1)} %get-tuple-element.41), channel_id=1, source_target_pairs={{0,5},{1,0},{4,1},{5,4},{2,7},{3,2},{6,3},{7,6},{8,13},{9,8},{12,9... | collective-permute-start | bytes 786440 | tf_op jit(solution)/shard_map/ppermute | solution.py:24
  150.3 12.3 %collective-permute-start.28 = (bf16[4,2,128,128]{3,2,1,0:T(8,128)(2,1)S(1)}, bf16[4,2,128,128]{3,2,1,0:T(8,128)(2,1)S(1)}, u32[]{:S(2)}, u32[]{:S(2)}) collective-permute-start(bf16[4,2,128,128]{3,2,1,0:T(8,128)(2,1)S(1)} %get-tuple-element.42), channel_id=1, source_target_pairs={{0,1},{1,4},{4,5},{5,0},{2,3},{3,6},{6,7},{7,2},{8,9},{9,12},{12,1... | collective-permute-start | bytes 786440 | tf_op jit(solution)/shard_map/ppermute | solution.py:24
  177.5 10.4 %collective-permute-start.30 = (bf16[128,128]{1,0:T(8,128)(2,1)S(1)}, bf16[128,128]{1,0:T(8,128)(2,1)S(1)}, u32[]{:S(2)}, u32[]{:S(2)}) collective-permute-start(bf16[128,128]{1,0:T(8,128)(2,1)S(1)} %reduce_sum.52), channel_id=1, source_target_pairs={{0,0},{16,64},{32,128},{48,192},{64,16},{80,80},{96,144},{112,208}... | collective-permute-start | bytes 98312 | tf_op jit(solution)/shard_map/ppermute | solution.py:386
  (13 other events, 91.4 us)
Sparse Core Ops, SparseCore 0:
  17.8 48.0 all-gather.1

commit v2 on v1

--- a/solution.py
+++ b/solution.py
@@ -92,26 +92,23 @@
 
 def teacher_kernel(
     ahead_ref, places_ref, mine_ref, other_ref, head_ref, code_ref, own_ref,
-    mine, head, chosen, acc, mine_sems, head_sems,
+    mine, other, head, chosen, acc, mine_sems, other_sems, head_sems,
 ):
     half, width = mine_ref.shape
     parts = head_sems.shape[0]
     tile = width // parts
     spans = [pl.ds(i * tile, tile) for i in range(parts)]
     got_mine = fetch([(mine_ref.at[:, span], mine.at[:, span]) for span in spans], mine_sems)
-    copies = fetch([(head_ref.at[span], head.at[span]) for span in spans], head_sems)
+    got_other = fetch([(other_ref.at[:, span], other.at[:, span]) for span in spans], other_sems)
     pick = (ahead_ref[...] == places_ref[...]).astype(f32).astype(bf16)
-
-    for copy in got_mine:
-        copy.wait()
-
-    @pl.loop(0, parts)
-    def _(i):
-        span = pl.ds(pl.multiple_of(i * tile, tile), tile)
+    for i, span in enumerate(spans):
+        got_mine[i].wait()
+        got_other[i].wait()
+        if i == 0:
+            copies = fetch([(head_ref.at[span], head.at[span]) for span in spans], head_sems)
         rows = jnp.dot(pick[:, :half], mine[:, span], preferred_element_type=f32)
-        rows += jnp.dot(pick[:, half:], other_ref[:, span], preferred_element_type=f32)
+        rows += jnp.dot(pick[:, half:], other[:, span], preferred_element_type=f32)
         chosen[:, span] = rows.astype(bf16)
-
     add_products(acc, chosen, head, copies)
     write_coded(acc, code_ref, own_ref)
 
@@ -128,14 +125,16 @@
     parts = 4
     return pl.pallas_call(
         teacher_kernel,
-        in_specs=in_vmem(2) + in_hbm(1) + in_vmem(1) + in_hbm(1),
+        in_specs=in_vmem(2) + in_hbm(3),
         out_specs=in_vmem(2),
         out_shape=coded_shapes(tokens // 4, cols),
         scratch_shapes=[
             pltpu.VMEM((half, width), bf16),
+            pltpu.VMEM((half, width), bf16),
             pltpu.VMEM((width, cols), bf16),
             pltpu.VMEM((tokens, width), bf16),
             pltpu.VMEM((tokens, cols), f32),
+            pltpu.SemaphoreType.DMA((parts,)),
             pltpu.SemaphoreType.DMA((parts,)),
             pltpu.SemaphoreType.DMA((parts,)),
         ],
@@ -146,7 +145,7 @@
             transcendentals=0,
         ),
         name="teacher_part",
-    )(ahead[:, None], places[None, :], stay(mine), other, stay(head))
+    )(ahead[:, None], places[None, :], stay(mine), stay(other), stay(head))
 
 
 def student_kernel(
@@ -336,7 +335,8 @@
     teacher_code, teacher_own = teacher_part(
         ahead, places.reshape(-1), rows, rows_other, teacher_head
     )
-    student_got, teacher_code = lax.optimization_barrier((student_got, teacher_code))
+    teacher_got = send_coded(teacher_code)
+    student_got, teacher_got[0] = lax.optimization_barrier((student_got, teacher_got[0]))
     student_logit = finish_sum(student_own, student_got)
 
     position = lax.broadcasted_iota(jnp.int32, (1, sampled.shape[0]), 1)
@@ -354,7 +354,7 @@
         ]
     )
     teacher_exp, teacher_sums = finish_teacher(
-        send_coded(teacher_code), teacher_own, student_logit, teacher_rest
+        teacher_got, teacher_own, student_logit, teacher_rest
     )
     sums = jnp.concatenate([teacher_sums, student_sums], 0)
     sums = lax.all_to_all(jnp.broadcast_to(sums[None], (64,) + sums.shape), VOCAB, 0, 0)

time: 196 us -> 192 us (0.980)
  waiting for transfers between devices: 69 us -> 64.6 us
  Pallas kernels: 22.6 us -> 18.9 us
  other arithmetic: 6.08 us -> 9.23 us
    ppermute x19, waiting for transfers between devices: 45 us -> 40.4 us  [shift(): return lax.ppermute(a, axes, [(i, (i + k) % n) for i in range(n)])]
    pallas_call x1, Pallas kernels: 12.9 us -> 9.17 us  [teacher_part(): pl.pallas_call(teacher_kernel, in_specs=in_vmem(2) + in_hbm(3), out_specs...]
    mul x3, other arithmetic: 0.03 us -> 2.07 us  [finish_sum(): scale = jnp.exp2(got[rows, :rows].astype(f32)) * (1.0 / TOP)]
  transfers between devices with their start and end apart: 32 -> 32, of which waited for: 21 -> 21; matrix products, arithmetic and copies ran while one was open for 3% -> 4% of each run, Pallas kernels for 10% -> 9%
where the time goes in v2:
time: 192 us; the launch traced here: 191 us
  waiting for transfers between devices  64.6 us (34%)
  starting transfers between devices  46.8 us (24%)
  blocking collectives  33.9 us (18%)
  Pallas kernels  18.9 us (10%)
  between operations  14.4 us (8%)
  other arithmetic  9.23 us (5%)
  local copies, waits for them, and re-layouts  3.6 us (2%)
    ppermute x19, waiting for transfers between devices, shift(): return lax.ppermute(a, axes, [(i, (i + k) % n) for i in range(n)])  40.4 us
    ppermute x19, starting transfers between devices, shift(): return lax.ppermute(a, axes, [(i, (i + k) % n) for i in range(n)])  30.9 us
    all_to_all x1, blocking collectives, per_device(): lax.all_to_all(jnp.broadcast_to(sums[None], (64,) + sums.shape), VOCAB, 0...  19.2 us
    all_to_all x1, blocking collectives, per_device(): lax.all_to_all(grad.astype(bf16).reshape(NZ, tok_rows, feats), Z, 0, 0)  14.7 us
    ppermute x4, starting transfers between devices, per_device(): lax.ppermute(got, ('y', 'zh'), swap_pairs(k))  11.4 us
    pallas_call x1, Pallas kernels, teacher_part(): pl.pallas_call(teacher_kernel, in_specs=in_vmem(2) + in_hbm(3), out_specs...  9.17 us
    ppermute x1, waiting for transfers between devices, per_device(): hidden_grad = lax.ppermute(grad, ('y', 'zh'), swap_pairs(0))  8.45 us
    ppermute x4, waiting for transfers between devices, per_device(): lax.ppermute(got, ('y', 'zh'), swap_pairs(k))  8.21 us
  transfers between devices with their start and end apart: 32, of which 21 were waited for; matrix products, arithmetic and copies ran while one was open for 4% of the time, Pallas kernels for 9%

profile of v2, /device:TPU:24, one launch (start us, length us, event | category | flops | bytes accessed | tf_op | source)
XLA Modules:
  0.0 191.4 jit_solution(2788179675842701476)
XLA Ops:
  7.2 3.1 %collective-permute-start.1 = (bf16[8,4096]{1,0:T(8,128)(2,1)}, bf16[8,4096]{1,0:T(8,128)(2,1)S(1)}, u32[]{:S(2)}, u32[]{:S(2)}) collective-permute-start(bf16[8,4096]{1,0:T(8,128)(2,1)} %param.9), channel_id=1, source_target_pairs={{0,4},{1,5},{4,0},{5,1},{2,6},{3,7},{6,2},{7,3},{8,12},{9,13},{12,... | collective-permute-start | bytes 196616 | tf_op jit(solution)/shard_map/ppermute | solution.py:24
  10.9 2.6 %collective-permute-start.2 = (bf16[8,4096]{1,0:T(8,128)(2,1)}, bf16[8,4096]{1,0:T(8,128)(2,1)S(1)}, u32[]{:S(2)}, u32[]{:S(2)}) collective-permute-start(bf16[8,4096]{1,0:T(8,128)(2,1)} %param.9), channel_id=1, source_target_pairs={{0,5},{1,0},{4,1},{5,4},{2,7},{3,2},{6,3},{7,6},{8,13},{9,8},{12,9... | collective-permute-start | bytes 196616 | tf_op jit(solution)/shard_map/ppermute | solution.py:24
  19.2 6.8 %collective-permute-start.4 = (bf16[2,128,128]{2,1,0:T(8,128)(2,1)S(1)}, bf16[2,128,128]{2,1,0:T(8,128)(2,1)S(1)}, u32[]{:S(2)}, u32[]{:S(2)}) collective-permute-start(bf16[2,128,128]{2,1,0:T(8,128)(2,1)S(1)} %pad_maximum_fusion.3), channel_id=1, source_target_pairs={{0,48},{16,112},{32,176},{48,240},{64,0},{80,64},{96,128},{112,192... | collective-permute-start | bytes 196616 | tf_op jit(solution)/shard_map/ppermute | solution.py:320
  26.1 4.0 %collective-permute-start.7 = (bf16[2,128,128]{2,1,0:T(8,128)(2,1)S(1)}, bf16[2,128,128]{2,1,0:T(8,128)(2,1)S(1)}, u32[]{:S(2)}, u32[]{:S(2)}) collective-permute-start(bf16[2,128,128]{2,1,0:T(8,128)(2,1)S(1)} %pad_maximum_fusion.3), channel_id=1, source_target_pairs={{0,0},{16,64},{32,128},{48,192},{64,16},{80,80},{96,144},{112,208}... | collective-permute-start | bytes 196616 | tf_op jit(solution)/shard_map/ppermute | solution.py:320
  30.7 8.2 %collective-permute-done.5 = bf16[2,128,128]{2,1,0:T(8,128)(2,1)S(1)} collective-permute-done((bf16[2,128,128]{2,1,0:T(8,128)(2,1)S(1)}, bf16[2,128,128]{2,1,0:T(8,128)(2,1)S(1)}, u32[]{:S(2)}, u32[]{:S(2)}) %collective-permute-start.5) | collective-permute-done | bytes 65568 | tf_op jit(solution)/shard_map/ppermute | solution.py:320
  39.1 3.6 %collective-permute-start.10 = (bf16[2,512,128]{2,1,0:T(8,128)(2,1)S(1)}, bf16[2,512,128]{2,1,0:T(8,128)(2,1)S(1)}, u32[]{:S(2)}, u32[]{:S(2)}) collective-permute-start(bf16[2,512,128]{2,1,0:T(8,128)(2,1)S(1)} %bitcast.88), channel_id=1, source_target_pairs={{0,5},{1,0},{4,1},{5,4},{2,7},{3,2},{6,3},{7,6},{8,13},{9,8},{12,9... | collective-permute-start | bytes 786440 | tf_op jit(solution)/shard_map/ppermute | solution.py:24
  44.4 2.8 %collective-permute-done.10 = bf16[2,512,128]{2,1,0:T(8,128)(2,1)S(1)} collective-permute-done((bf16[2,512,128]{2,1,0:T(8,128)(2,1)S(1)}, bf16[2,512,128]{2,1,0:T(8,128)(2,1)S(1)}, u32[]{:S(2)}, u32[]{:S(2)}) %collective-permute-start.10) | collective-permute-done | bytes 262176 | tf_op jit(solution)/shard_map/ppermute | solution.py:24
  47.3 5.9 %collective-permute-done.9 = bf16[2,512,128]{2,1,0:T(8,128)(2,1)S(1)} collective-permute-done((bf16[2,512,128]{2,1,0:T(8,128)(2,1)S(1)}, bf16[2,512,128]{2,1,0:T(8,128)(2,1)S(1)}, u32[]{:S(2)}, u32[]{:S(2)}) %collective-permute-start.9) | collective-permute-done | bytes 262176 | tf_op jit(solution)/shard_map/ppermute | solution.py:24
  55.2 5.4 %student_part.1 = (s16[3,144,1024]{2,1,0:T(8,128)(2,1)S(1)}, f32[128,1024]{1,0:T(8,128)S(1)}) custom-call(s32[16]{0:T(128)S(1)} %add.248.order_ref, bf16[8,512,128]{2,1,0:T(8,128)(2,1)S(1)} %pad_maximum_fusion.mine_ref, bf16[8,512,128]{2,1,0:T(8,128)(2,1)S(1)} %pad_maximum_fusion.1.other_ref, bf16[2048,1024]{1,0:T(8,128)(2,1)} %head_ref.7), custom_call_target="tpu_custom_call" | custom-call | flops 2147483648 | bytes 6291456 | tf_op jit(solution)/shard_map/student_part/pallas_call | solution.py:170
  60.6 5.3 %all-gather.2.cloned.1.call-done.mine_ref = bf16[256,4096]{1,0:T(8,128)(2,1)} async-done(((bf16[32,4096]{1,0:T(8,128)(2,1)}), bf16[256,4096]{1,0:T(8,128)(2,1)}) %all-gather.2.cloned.1.call-update) | async-done | bytes 2097168 | tf_op jit(solution)/shard_map/all_gather | solution.py:317
  70.4 9.2 %teacher_part.1 = (s16[3,144,1024]{2,1,0:T(8,128)(2,1)S(1)}, f32[128,1024]{1,0:T(8,128)S(1)}) custom-call(s32[512,1]{1,0:T(8,128)S(1)} %copy.18.ahead_ref, s32[1,512]{1,0:T(1,128)S(1)} %add.265.places_ref, bf16[256,4096]{1,0:T(8,128)(2,1)} %all-gather.2.cloned.1.call-done.mine_ref, bf16[256,4096]{1,0:T(8,128)(2,1)} %collective-permute-done.18.other_ref, ...), custom_call_target="tpu_custom_call" | custom-call | flops 6442450944 | bytes 12582912 | tf_op jit(solution)/shard_map/teacher_part/pallas_call | solution.py:126
  79.6 3.0 %collective-permute-start.19 = (s16[144,1024]{1,0:T(8,128)(2,1)S(1)}, s16[144,1024]{1,0:T(8,128)(2,1)S(1)}, u32[]{:S(2)}, u32[]{:S(2)}) collective-permute-start(s16[144,1024]{1,0:T(8,128)(2,1)S(1)} %get-tuple-element.45), channel_id=1, source_target_pairs={{0,128},{64,192},{128,0},{192,64},{1,129},{65,193},{129,1},{193,65... | collective-permute-start | bytes 884744 | tf_op jit(solution)/shard_map/ppermute | solution.py:24
  83.6 2.8 %collective-permute-start.20 = (s16[144,1024]{1,0:T(8,128)(2,1)S(1)}, s16[144,1024]{1,0:T(8,128)(2,1)S(1)}, u32[]{:S(2)}, u32[]{:S(2)}) collective-permute-start(s16[144,1024]{1,0:T(8,128)(2,1)S(1)} %get-tuple-element.44), channel_id=1, source_target_pairs={{0,64},{64,128},{128,192},{192,0},{1,65},{65,129},{129,193},{193,1... | collective-permute-start | bytes 884744 | tf_op jit(solution)/shard_map/ppermute | solution.py:24
  86.4 2.7 %collective-permute-done.16 = s16[144,1024]{1,0:T(8,128)(2,1)} collective-permute-done((s16[144,1024]{1,0:T(8,128)(2,1)S(1)}, s16[144,1024]{1,0:T(8,128)(2,1)}, u32[]{:S(2)}, u32[]{:S(2)}) %collective-permute-start.16) | collective-permute-done | bytes 294944 | tf_op jit(solution)/shard_map/ppermute | solution.py:24
  97.2 19.2 %all_to_all.10 = f32[64,4,128]{2,1,0:T(4,128)S(1)} all-to-all(f32[64,4,128]{2,1,0:T(4,128)S(1)} %broadcast_in_dim.27), channel_id=1, replica_groups=mesh['y'=4,'zh'=4,'zl'=2,'xh'=2,'c'=2,'xl'=2] {'zh','zl','xh','c','xl'}, dimensions={0} | all-to-all | bytes 262144 | tf_op jit(solution)/shard_map/all_to_all | solution.py:360
  117.2 2.6 %collective-permute-start.23 = (bf16[128,1024]{1,0:T(8,128)(2,1)S(1)}, bf16[128,1024]{1,0:T(8,128)(2,1)S(1)}, u32[]{:S(2)}, u32[]{:S(2)}) collective-permute-start(bf16[128,1024]{1,0:T(8,128)(2,1)S(1)} %multiply_convert_fusion.own_ref), channel_id=1, source_target_pairs={{0,64},{64,128},{128,192},{192,0},{1,65},{65,129},{129,193},{193,1... | collective-permute-start | bytes 786440 | tf_op jit(solution)/shard_map/ppermute | solution.py:24
  119.8 5.9 %collective-permute-done.23.behind_ref = bf16[128,1024]{1,0:T(8,128)(2,1)S(1)} collective-permute-done((bf16[128,1024]{1,0:T(8,128)(2,1)S(1)}, bf16[128,1024]{1,0:T(8,128)(2,1)S(1)}, u32[]{:S(2)}, u32[]{:S(2)}) %collective-permute-start.23) | collective-permute-done | bytes 262176 | tf_op jit(solution)/shard_map/ppermute | solution.py:24
  125.7 3.8 %collective-permute-start.24 = (bf16[64,1024]{1,0:T(8,128)(2,1)S(1)}, bf16[64,1024]{1,0:T(8,128)(2,1)S(1)}, u32[]{:S(2)}, u32[]{:S(2)}) collective-permute-start(bf16[64,1024]{1,0:T(8,128)(2,1)S(1)} %slice.79), channel_id=1, source_target_pairs={{0,64},{64,128},{128,192},{192,0},{1,65},{65,129},{129,193},{193,1... | collective-permute-start | bytes 393224 | tf_op jit(solution)/shard_map/ppermute | solution.py:24
  132.0 3.8 %collective-permute-done.25.far1_ref = bf16[64,1024]{1,0:T(8,128)(2,1)S(1)} collective-permute-done((bf16[64,1024]{1,0:T(8,128)(2,1)S(1)}, bf16[64,1024]{1,0:T(8,128)(2,1)S(1)}, u32[]{:S(2)}, u32[]{:S(2)}) %collective-permute-start.25) | collective-permute-done | bytes 131104 | tf_op jit(solution)/shard_map/ppermute | solution.py:24
  143.5 2.8 %collective-permute-start.29 = (bf16[4,2,128,128]{3,2,1,0:T(8,128)(2,1)S(1)}, bf16[4,2,128,128]{3,2,1,0:T(8,128)(2,1)S(1)}, u32[]{:S(2)}, u32[]{:S(2)}) collective-permute-start(bf16[4,2,128,128]{3,2,1,0:T(8,128)(2,1)S(1)} %get-tuple-element.41), channel_id=1, source_target_pairs={{0,5},{1,0},{4,1},{5,4},{2,7},{3,2},{6,3},{7,6},{8,13},{9,8},{12,9... | collective-permute-start | bytes 786440 | tf_op jit(solution)/shard_map/ppermute | solution.py:24
  146.3 7.5 %collective-permute-done.27 = bf16[4,2,128,128]{3,2,1,0:T(8,128)(2,1)S(1)} collective-permute-done((bf16[4,2,128,128]{3,2,1,0:T(8,128)(2,1)S(1)}, bf16[4,2,128,128]{3,2,1,0:T(8,128)(2,1)S(1)}, u32[]{:S(2)}, u32[]{:S(2)}) %collective-permute-start.27) | collective-permute-done | bytes 262176 | tf_op jit(solution)/shard_map/ppermute | solution.py:24
  153.8 2.7 %collective-permute-done.29 = bf16[4,2,128,128]{3,2,1,0:T(8,128)(2,1)S(1)} collective-permute-done((bf16[4,2,128,128]{3,2,1,0:T(8,128)(2,1)S(1)}, bf16[4,2,128,128]{3,2,1,0:T(8,128)(2,1)S(1)}, u32[]{:S(2)}, u32[]{:S(2)}) %collective-permute-start.29) | collective-permute-done | bytes 262176 | tf_op jit(solution)/shard_map/ppermute | solution.py:24
  158.8 14.7 %all_to_all.11 = bf16[8,128,128]{2,1,0:T(8,128)(2,1)S(1)} all-to-all(bf16[8,128,128]{2,1,0:T(8,128)(2,1)S(1)} %bitcast.87), channel_id=1, replica_groups=mesh['y'=4,'zh'=4,'zl'=2,'xh'=2,'c'=2,'xl'=2] {'zh','zl'}, dimensions={0} | all-to-all | bytes 524288 | tf_op jit(solution)/shard_map/all_to_all | solution.py:384
  175.5 8.4 %collective-permute-done.30 = bf16[128,128]{1,0:T(8,128)(2,1)S(1)} collective-permute-done((bf16[128,128]{1,0:T(8,128)(2,1)S(1)}, bf16[128,128]{1,0:T(8,128)(2,1)S(1)}, u32[]{:S(2)}, u32[]{:S(2)}) %collective-permute-start.30) | collective-permute-done | bytes 32800 | tf_op jit(solution)/shard_map/ppermute | solution.py:386
  (110 shorter events, 40.1 us)
Async XLA Ops:
  7.2 58.7 %all-gather.2.cloned.1.call-start = ((), (), s32[]{:S(2)}) async-start(), calls=%async_computation.2 | async-start | bytes 2359296 | tf_op jit(solution)/shard_map/all_gather | solution.py:317
  7.2 8.3 %collective-permute-start.1 = (bf16[8,4096]{1,0:T(8,128)(2,1)}, bf16[8,4096]{1,0:T(8,128)(2,1)S(1)}, u32[]{:S(2)}, u32[]{:S(2)}) collective-permute-start(bf16[8,4096]{1,0:T(8,128)(2,1)} %param.9), channel_id=1, source_target_pairs={{0,4},{1,5},{4,0},{5,1},{2,6},{3,7},{6,2},{7,3},{8,12},{9,13},{12,... | collective-permute-start | bytes 196616 | tf_op jit(solution)/shard_map/ppermute | solution.py:24
  19.2 11.5 %collective-permute-start.4 = (bf16[2,128,128]{2,1,0:T(8,128)(2,1)S(1)}, bf16[2,128,128]{2,1,0:T(8,128)(2,1)S(1)}, u32[]{:S(2)}, u32[]{:S(2)}) collective-permute-start(bf16[2,128,128]{2,1,0:T(8,128)(2,1)S(1)} %pad_maximum_fusion.3), channel_id=1, source_target_pairs={{0,48},{16,112},{32,176},{48,240},{64,0},{80,64},{96,128},{112,192... | collective-permute-start | bytes 196616 | tf_op jit(solution)/shard_map/ppermute | solution.py:320
  26.1 12.8 %collective-permute-start.7 = (bf16[2,128,128]{2,1,0:T(8,128)(2,1)S(1)}, bf16[2,128,128]{2,1,0:T(8,128)(2,1)S(1)}, u32[]{:S(2)}, u32[]{:S(2)}) collective-permute-start(bf16[2,128,128]{2,1,0:T(8,128)(2,1)S(1)} %pad_maximum_fusion.3), channel_id=1, source_target_pairs={{0,0},{16,64},{32,128},{48,192},{64,16},{80,80},{96,144},{112,208}... | collective-permute-start | bytes 196616 | tf_op jit(solution)/shard_map/ppermute | solution.py:320
  30.2 8.8 %collective-permute-start.6 = (bf16[2,128,128]{2,1,0:T(8,128)(2,1)S(1)}, bf16[2,128,128]{2,1,0:T(8,128)(2,1)S(1)}, u32[]{:S(2)}, u32[]{:S(2)}) collective-permute-start(bf16[2,128,128]{2,1,0:T(8,128)(2,1)S(1)} %pad_maximum_fusion.3), channel_id=1, source_target_pairs={{0,16},{16,80},{32,144},{48,208},{64,32},{80,96},{96,160},{112,224... | collective-permute-start | bytes 196616 | tf_op jit(solution)/shard_map/ppermute | solution.py:320
  30.2 8.7 %collective-permute-start.5 = (bf16[2,128,128]{2,1,0:T(8,128)(2,1)S(1)}, bf16[2,128,128]{2,1,0:T(8,128)(2,1)S(1)}, u32[]{:S(2)}, u32[]{:S(2)}) collective-permute-start(bf16[2,128,128]{2,1,0:T(8,128)(2,1)S(1)} %pad_maximum_fusion.3), channel_id=1, source_target_pairs={{0,32},{16,96},{32,160},{48,224},{64,48},{80,112},{96,176},{112,24... | collective-permute-start | bytes 196616 | tf_op jit(solution)/shard_map/ppermute | solution.py:320
  39.1 8.1 %collective-permute-start.10 = (bf16[2,512,128]{2,1,0:T(8,128)(2,1)S(1)}, bf16[2,512,128]{2,1,0:T(8,128)(2,1)S(1)}, u32[]{:S(2)}, u32[]{:S(2)}) collective-permute-start(bf16[2,512,128]{2,1,0:T(8,128)(2,1)S(1)} %bitcast.88), channel_id=1, source_target_pairs={{0,5},{1,0},{4,1},{5,4},{2,7},{3,2},{6,3},{7,6},{8,13},{9,8},{12,9... | collective-permute-start | bytes 786440 | tf_op jit(solution)/shard_map/ppermute | solution.py:24
  42.7 10.4 %collective-permute-start.9 = (bf16[2,512,128]{2,1,0:T(8,128)(2,1)S(1)}, bf16[2,512,128]{2,1,0:T(8,128)(2,1)S(1)}, u32[]{:S(2)}, u32[]{:S(2)}) collective-permute-start(bf16[2,512,128]{2,1,0:T(8,128)(2,1)S(1)} %bitcast.89), channel_id=1, source_target_pairs={{0,1},{1,4},{4,5},{5,0},{2,3},{3,6},{6,7},{7,2},{8,9},{9,12},{12,1... | collective-permute-start | bytes 786440 | tf_op jit(solution)/shard_map/ppermute | solution.py:24
  42.7 10.4 %collective-permute-start.8 = (bf16[2,512,128]{2,1,0:T(8,128)(2,1)S(1)}, bf16[2,512,128]{2,1,0:T(8,128)(2,1)S(1)}, u32[]{:S(2)}, u32[]{:S(2)}) collective-permute-start(bf16[2,512,128]{2,1,0:T(8,128)(2,1)S(1)} %bitcast.90), channel_id=1, source_target_pairs={{0,4},{1,5},{4,0},{5,1},{2,6},{3,7},{6,2},{7,3},{8,12},{9,13},{12,... | collective-permute-start | bytes 786440 | tf_op jit(solution)/shard_map/ppermute | solution.py:24
  44.4 9.5 %collective-permute-start.11 = (bf16[2,512,128]{2,1,0:T(8,128)(2,1)S(1)}, bf16[2,512,128]{2,1,0:T(8,128)(2,1)S(1)}, u32[]{:S(2)}, u32[]{:S(2)}) collective-permute-start(bf16[2,512,128]{2,1,0:T(8,128)(2,1)S(1)} %bitcast.91), channel_id=1, source_target_pairs={{0,2},{2,0},{1,3},{3,1},{4,6},{6,4},{5,7},{7,5},{8,10},{10,8},{9,1... | collective-permute-start | bytes 786440 | tf_op jit(solution)/shard_map/ppermute | solution.py:28
  47.3 6.7 %collective-permute-start.14 = (bf16[2,512,128]{2,1,0:T(8,128)(2,1)S(1)}, bf16[2,512,128]{2,1,0:T(8,128)(2,1)S(1)}, u32[]{:S(2)}, u32[]{:S(2)}) collective-permute-start(bf16[2,512,128]{2,1,0:T(8,128)(2,1)S(1)} %collective-permute-done.10), channel_id=1, source_target_pairs={{0,2},{2,0},{1,3},{3,1},{4,6},{6,4},{5,7},{7,5},{8,10},{10,8},{9,1... | collective-permute-start | bytes 786440 | tf_op jit(solution)/shard_map/ppermute | solution.py:28
  66.5 17.1 %collective-permute-start.17 = (s16[144,1024]{1,0:T(8,128)(2,1)S(1)}, s16[144,1024]{1,0:T(8,128)(2,1)}, u32[]{:S(2)}, u32[]{:S(2)}) collective-permute-start(s16[144,1024]{1,0:T(8,128)(2,1)S(1)} %get-tuple-element.46), channel_id=1, source_target_pairs={{0,192},{64,0},{128,64},{192,128},{1,193},{65,1},{129,65},{193,129... | collective-permute-start | bytes 884744 | tf_op jit(solution)/shard_map/ppermute | solution.py:24
  67.8 21.3 %collective-permute-start.16 = (s16[144,1024]{1,0:T(8,128)(2,1)S(1)}, s16[144,1024]{1,0:T(8,128)(2,1)}, u32[]{:S(2)}, u32[]{:S(2)}) collective-permute-start(s16[144,1024]{1,0:T(8,128)(2,1)S(1)} %get-tuple-element.47), channel_id=1, source_target_pairs={{0,64},{64,128},{128,192},{192,0},{1,65},{65,129},{129,193},{193,1... | collective-permute-start | bytes 884744 | tf_op jit(solution)/shard_map/ppermute | solution.py:24
  69.8 19.3 %collective-permute-start.15 = (s16[144,1024]{1,0:T(8,128)(2,1)S(1)}, s16[144,1024]{1,0:T(8,128)(2,1)}, u32[]{:S(2)}, u32[]{:S(2)}) collective-permute-start(s16[144,1024]{1,0:T(8,128)(2,1)S(1)} %get-tuple-element.48), channel_id=1, source_target_pairs={{0,128},{64,192},{128,0},{192,64},{1,129},{65,193},{129,1},{193,65... | collective-permute-start | bytes 884744 | tf_op jit(solution)/shard_map/ppermute | solution.py:24
  79.6 11.5 %collective-permute-start.19 = (s16[144,1024]{1,0:T(8,128)(2,1)S(1)}, s16[144,1024]{1,0:T(8,128)(2,1)S(1)}, u32[]{:S(2)}, u32[]{:S(2)}) collective-permute-start(s16[144,1024]{1,0:T(8,128)(2,1)S(1)} %get-tuple-element.45), channel_id=1, source_target_pairs={{0,128},{64,192},{128,0},{192,64},{1,129},{65,193},{129,1},{193,65... | collective-permute-start | bytes 884744 | tf_op jit(solution)/shard_map/ppermute | solution.py:24
  82.9 13.7 %collective-permute-start.21 = (s16[144,1024]{1,0:T(8,128)(2,1)S(1)}, s16[144,1024]{1,0:T(8,128)(2,1)S(1)}, u32[]{:S(2)}, u32[]{:S(2)}) collective-permute-start(s16[144,1024]{1,0:T(8,128)(2,1)S(1)} %get-tuple-element.43), channel_id=1, source_target_pairs={{0,192},{64,0},{128,64},{192,128},{1,193},{65,1},{129,65},{193,129... | collective-permute-start | bytes 884744 | tf_op jit(solution)/shard_map/ppermute | solution.py:24
  83.6 13.0 %collective-permute-start.20 = (s16[144,1024]{1,0:T(8,128)(2,1)S(1)}, s16[144,1024]{1,0:T(8,128)(2,1)S(1)}, u32[]{:S(2)}, u32[]{:S(2)}) collective-permute-start(s16[144,1024]{1,0:T(8,128)(2,1)S(1)} %get-tuple-element.44), channel_id=1, source_target_pairs={{0,64},{64,128},{128,192},{192,0},{1,65},{65,129},{129,193},{193,1... | collective-permute-start | bytes 884744 | tf_op jit(solution)/shard_map/ppermute | solution.py:24
  117.2 8.5 %collective-permute-start.23 = (bf16[128,1024]{1,0:T(8,128)(2,1)S(1)}, bf16[128,1024]{1,0:T(8,128)(2,1)S(1)}, u32[]{:S(2)}, u32[]{:S(2)}) collective-permute-start(bf16[128,1024]{1,0:T(8,128)(2,1)S(1)} %multiply_convert_fusion.own_ref), channel_id=1, source_target_pairs={{0,64},{64,128},{128,192},{192,0},{1,65},{65,129},{129,193},{193,1... | collective-permute-start | bytes 786440 | tf_op jit(solution)/shard_map/ppermute | solution.py:24
  119.8 9.7 %collective-permute-start.22 = (bf16[128,1024]{1,0:T(8,128)(2,1)S(1)}, bf16[128,1024]{1,0:T(8,128)(2,1)S(1)}, u32[]{:S(2)}, u32[]{:S(2)}) collective-permute-start(bf16[128,1024]{1,0:T(8,128)(2,1)S(1)} %multiply_convert_fusion.own_ref), channel_id=1, source_target_pairs={{0,192},{64,0},{128,64},{192,128},{1,193},{65,1},{129,65},{193,129... | collective-permute-start | bytes 786440 | tf_op jit(solution)/shard_map/ppermute | solution.py:24
  125.7 6.3 %collective-permute-start.24 = (bf16[64,1024]{1,0:T(8,128)(2,1)S(1)}, bf16[64,1024]{1,0:T(8,128)(2,1)S(1)}, u32[]{:S(2)}, u32[]{:S(2)}) collective-permute-start(bf16[64,1024]{1,0:T(8,128)(2,1)S(1)} %slice.79), channel_id=1, source_target_pairs={{0,64},{64,128},{128,192},{192,0},{1,65},{65,129},{129,193},{193,1... | collective-permute-start | bytes 393224 | tf_op jit(solution)/shard_map/ppermute | solution.py:24
  143.1 10.8 %collective-permute-start.27 = (bf16[4,2,128,128]{3,2,1,0:T(8,128)(2,1)S(1)}, bf16[4,2,128,128]{3,2,1,0:T(8,128)(2,1)S(1)}, u32[]{:S(2)}, u32[]{:S(2)}) collective-permute-start(bf16[4,2,128,128]{3,2,1,0:T(8,128)(2,1)S(1)} %get-tuple-element.40), channel_id=1, source_target_pairs={{0,4},{1,5},{4,0},{5,1},{2,6},{3,7},{6,2},{7,3},{8,12},{9,13},{12,... | collective-permute-start | bytes 786440 | tf_op jit(solution)/shard_map/ppermute | solution.py:24
  143.5 13.1 %collective-permute-start.29 = (bf16[4,2,128,128]{3,2,1,0:T(8,128)(2,1)S(1)}, bf16[4,2,128,128]{3,2,1,0:T(8,128)(2,1)S(1)}, u32[]{:S(2)}, u32[]{:S(2)}) collective-permute-start(bf16[4,2,128,128]{3,2,1,0:T(8,128)(2,1)S(1)} %get-tuple-element.41), channel_id=1, source_target_pairs={{0,5},{1,0},{4,1},{5,4},{2,7},{3,2},{6,3},{7,6},{8,13},{9,8},{12,9... | collective-permute-start | bytes 786440 | tf_op jit(solution)/shard_map/ppermute | solution.py:24
  146.3 12.3 %collective-permute-start.28 = (bf16[4,2,128,128]{3,2,1,0:T(8,128)(2,1)S(1)}, bf16[4,2,128,128]{3,2,1,0:T(8,128)(2,1)S(1)}, u32[]{:S(2)}, u32[]{:S(2)}) collective-permute-start(bf16[4,2,128,128]{3,2,1,0:T(8,128)(2,1)S(1)} %get-tuple-element.42), channel_id=1, source_target_pairs={{0,1},{1,4},{4,5},{5,0},{2,3},{3,6},{6,7},{7,2},{8,9},{9,12},{12,1... | collective-permute-start | bytes 786440 | tf_op jit(solution)/shard_map/ppermute | solution.py:24
  173.6 10.4 %collective-permute-start.30 = (bf16[128,128]{1,0:T(8,128)(2,1)S(1)}, bf16[128,128]{1,0:T(8,128)(2,1)S(1)}, u32[]{:S(2)}, u32[]{:S(2)}) collective-permute-start(bf16[128,128]{1,0:T(8,128)(2,1)S(1)} %reduce_sum.52), channel_id=1, source_target_pairs={{0,0},{16,64},{32,128},{48,192},{64,16},{80,80},{96,144},{112,208}... | collective-permute-start | bytes 98312 | tf_op jit(solution)/shard_map/ppermute | solution.py:386
  (13 other events, 98.4 us)
Sparse Core Ops, SparseCore 0:
  17.8 48.0 all-gather.1

commit v3 on v2

--- a/solution.py
+++ b/solution.py
@@ -188,6 +188,26 @@
     )(order, mine, other, stay(head))
 
 
+def bring_kernel(head_ref, out_ref, sems):
+    for copy in fetch([(head_ref, out_ref)], sems):
+        copy.wait()
+
+
+def bring(head):
+    return pl.pallas_call(
+        bring_kernel,
+        in_specs=in_hbm(1),
+        out_specs=pl.BlockSpec(memory_space=pl.ANY),
+        out_shape=jax.ShapeDtypeStruct(head.shape, head.dtype),
+        scratch_shapes=[pltpu.SemaphoreType.DMA((1,))],
+        compiler_params=pltpu.CompilerParams(vmem_limit_bytes=1024 * 1024),
+        cost_estimate=pl.CostEstimate(
+            flops=0, bytes_accessed=4 * head.shape[0] * head.shape[1], transcendentals=0
+        ),
+        name="bring",
+    )(stay(head))
+
+
 def gradient_kernel(
     where_ref, own_ref, front_ref, far0_ref, far1_ref, behind_ref, head_ref, out_ref,
     delta,
@@ -370,6 +390,8 @@
         loss_scale * (student_exp * student_scale[:, None] - teacher_exp * teacher_scale[:, None])
     ).astype(bf16)
     half = tok_rows // 2
+    delta, student_head = lax.optimization_barrier((delta, student_head))
+    student_head = bring(student_head)
     behind = shift(delta, "y", NY, 1)
     front = shift(delta, "y", NY, -1)
     far = [shift(behind[:half], "y", NY, 1), shift(front[half:], "y", NY, -1)]

time: 192 us -> 190 us (0.990)
  Pallas kernels: 18.9 us -> 21.1 us
  waiting for transfers between devices: 64.6 us -> 62.4 us
  local copies, waits for them, and re-layouts: 3.6 us -> 1.41 us
    pallas_call x0 -> x1, Pallas kernels: none -> 2.2 us  [bring(): pl.pallas_call(bring_kernel, in_specs=in_hbm(1), out_specs=pl.BlockSpec(m...]
    unnamed x18 -> x16, local copies, waits for them, and re-layouts: 2.91 us -> 0.73 us
    ppermute x19, waiting for transfers between devices: 40.4 us -> 38.2 us  [shift(): return lax.ppermute(a, axes, [(i, (i + k) % n) for i in range(n)])]
  transfers between devices with their start and end apart: 32 -> 32, of which waited for: 21 -> 21; matrix products, arithmetic and copies ran while one was open for 4% -> 4% of each run, Pallas kernels for 9% -> 10%
where the time goes in v3:
time: 190 us; the launch traced here: 189 us
  waiting for transfers between devices  62.4 us (33%)
  starting transfers between devices  46.8 us (25%)
  blocking collectives  33.9 us (18%)
  Pallas kernels  21.1 us (11%)
  between operations  14.4 us (8%)
  other arithmetic  9.21 us (5%)
    ppermute x19, waiting for transfers between devices, shift(): return lax.ppermute(a, axes, [(i, (i + k) % n) for i in range(n)])  38.2 us
    ppermute x19, starting transfers between devices, shift(): return lax.ppermute(a, axes, [(i, (i + k) % n) for i in range(n)])  30.9 us
    all_to_all x1, blocking collectives, per_device(): lax.all_to_all(jnp.broadcast_to(sums[None], (64,) + sums.shape), VOCAB, 0...  19.2 us
    all_to_all x1, blocking collectives, per_device(): lax.all_to_all(grad.astype(bf16).reshape(NZ, tok_rows, feats), Z, 0, 0)  14.7 us
    ppermute x4, starting transfers between devices, per_device(): lax.ppermute(got, ('y', 'zh'), swap_pairs(k))  11.4 us
    pallas_call x1, Pallas kernels, teacher_part(): pl.pallas_call(teacher_kernel, in_specs=in_vmem(2) + in_hbm(3), out_specs...  9.17 us
    ppermute x1, waiting for transfers between devices, per_device(): hidden_grad = lax.ppermute(grad, ('y', 'zh'), swap_pairs(0))  8.45 us
    ppermute x4, waiting for transfers between devices, per_device(): lax.ppermute(got, ('y', 'zh'), swap_pairs(k))  8.2 us
  transfers between devices with their start and end apart: 32, of which 21 were waited for; matrix products, arithmetic and copies ran while one was open for 4% of the time, Pallas kernels for 10%

profile of v3, /device:TPU:24, one launch (start us, length us, event | category | flops | bytes accessed | tf_op | source)
XLA Modules:
  0.0 189.2 jit_solution(8674543999427689799)
XLA Ops:
  7.2 3.1 %collective-permute-start.1 = (bf16[8,4096]{1,0:T(8,128)(2,1)}, bf16[8,4096]{1,0:T(8,128)(2,1)S(1)}, u32[]{:S(2)}, u32[]{:S(2)}) collective-permute-start(bf16[8,4096]{1,0:T(8,128)(2,1)} %param.9), channel_id=1, source_target_pairs={{0,4},{1,5},{4,0},{5,1},{2,6},{3,7},{6,2},{7,3},{8,12},{9,13},{12,... | collective-permute-start | bytes 196616 | tf_op jit(solution)/shard_map/ppermute | solution.py:24
  10.9 2.6 %collective-permute-start.2 = (bf16[8,4096]{1,0:T(8,128)(2,1)}, bf16[8,4096]{1,0:T(8,128)(2,1)S(1)}, u32[]{:S(2)}, u32[]{:S(2)}) collective-permute-start(bf16[8,4096]{1,0:T(8,128)(2,1)} %param.9), channel_id=1, source_target_pairs={{0,5},{1,0},{4,1},{5,4},{2,7},{3,2},{6,3},{7,6},{8,13},{9,8},{12,9... | collective-permute-start | bytes 196616 | tf_op jit(solution)/shard_map/ppermute | solution.py:24
  19.2 6.8 %collective-permute-start.4 = (bf16[2,128,128]{2,1,0:T(8,128)(2,1)S(1)}, bf16[2,128,128]{2,1,0:T(8,128)(2,1)S(1)}, u32[]{:S(2)}, u32[]{:S(2)}) collective-permute-start(bf16[2,128,128]{2,1,0:T(8,128)(2,1)S(1)} %pad_maximum_fusion.3), channel_id=1, source_target_pairs={{0,48},{16,112},{32,176},{48,240},{64,0},{80,64},{96,128},{112,192... | collective-permute-start | bytes 196616 | tf_op jit(solution)/shard_map/ppermute | solution.py:340
  26.1 4.0 %collective-permute-start.7 = (bf16[2,128,128]{2,1,0:T(8,128)(2,1)S(1)}, bf16[2,128,128]{2,1,0:T(8,128)(2,1)S(1)}, u32[]{:S(2)}, u32[]{:S(2)}) collective-permute-start(bf16[2,128,128]{2,1,0:T(8,128)(2,1)S(1)} %pad_maximum_fusion.3), channel_id=1, source_target_pairs={{0,0},{16,64},{32,128},{48,192},{64,16},{80,80},{96,144},{112,208}... | collective-permute-start | bytes 196616 | tf_op jit(solution)/shard_map/ppermute | solution.py:340
  30.7 8.2 %collective-permute-done.5 = bf16[2,128,128]{2,1,0:T(8,128)(2,1)S(1)} collective-permute-done((bf16[2,128,128]{2,1,0:T(8,128)(2,1)S(1)}, bf16[2,128,128]{2,1,0:T(8,128)(2,1)S(1)}, u32[]{:S(2)}, u32[]{:S(2)}) %collective-permute-start.5) | collective-permute-done | bytes 65568 | tf_op jit(solution)/shard_map/ppermute | solution.py:340
  39.1 3.6 %collective-permute-start.10 = (bf16[2,512,128]{2,1,0:T(8,128)(2,1)S(1)}, bf16[2,512,128]{2,1,0:T(8,128)(2,1)S(1)}, u32[]{:S(2)}, u32[]{:S(2)}) collective-permute-start(bf16[2,512,128]{2,1,0:T(8,128)(2,1)S(1)} %bitcast.88), channel_id=1, source_target_pairs={{0,5},{1,0},{4,1},{5,4},{2,7},{3,2},{6,3},{7,6},{8,13},{9,8},{12,9... | collective-permute-start | bytes 786440 | tf_op jit(solution)/shard_map/ppermute | solution.py:24
  44.4 2.8 %collective-permute-done.10 = bf16[2,512,128]{2,1,0:T(8,128)(2,1)S(1)} collective-permute-done((bf16[2,512,128]{2,1,0:T(8,128)(2,1)S(1)}, bf16[2,512,128]{2,1,0:T(8,128)(2,1)S(1)}, u32[]{:S(2)}, u32[]{:S(2)}) %collective-permute-start.10) | collective-permute-done | bytes 262176 | tf_op jit(solution)/shard_map/ppermute | solution.py:24
  47.3 5.8 %collective-permute-done.9 = bf16[2,512,128]{2,1,0:T(8,128)(2,1)S(1)} collective-permute-done((bf16[2,512,128]{2,1,0:T(8,128)(2,1)S(1)}, bf16[2,512,128]{2,1,0:T(8,128)(2,1)S(1)}, u32[]{:S(2)}, u32[]{:S(2)}) %collective-permute-start.9) | collective-permute-done | bytes 262176 | tf_op jit(solution)/shard_map/ppermute | solution.py:24
  55.2 5.4 %student_part.1 = (s16[3,144,1024]{2,1,0:T(8,128)(2,1)S(1)}, f32[128,1024]{1,0:T(8,128)S(1)}) custom-call(s32[16]{0:T(128)S(1)} %add.248.order_ref, bf16[8,512,128]{2,1,0:T(8,128)(2,1)S(1)} %pad_maximum_fusion.mine_ref, bf16[8,512,128]{2,1,0:T(8,128)(2,1)S(1)} %pad_maximum_fusion.1.other_ref, bf16[2048,1024]{1,0:T(8,128)(2,1)} %head_ref.4), custom_call_target="tpu_custom_call" | custom-call | flops 2147483648 | bytes 6291456 | tf_op jit(solution)/shard_map/student_part/pallas_call | solution.py:170
  60.6 5.3 %all-gather.2.cloned.1.call-done.mine_ref = bf16[256,4096]{1,0:T(8,128)(2,1)} async-done(((bf16[32,4096]{1,0:T(8,128)(2,1)}), bf16[256,4096]{1,0:T(8,128)(2,1)}) %all-gather.2.cloned.1.call-update) | async-done | bytes 2097168 | tf_op jit(solution)/shard_map/all_gather | solution.py:337
  70.4 9.2 %teacher_part.1 = (s16[3,144,1024]{2,1,0:T(8,128)(2,1)S(1)}, f32[128,1024]{1,0:T(8,128)S(1)}) custom-call(s32[512,1]{1,0:T(8,128)S(1)} %copy.18.ahead_ref, s32[1,512]{1,0:T(1,128)S(1)} %add.265.places_ref, bf16[256,4096]{1,0:T(8,128)(2,1)} %all-gather.2.cloned.1.call-done.mine_ref, bf16[256,4096]{1,0:T(8,128)(2,1)} %collective-permute-done.18.other_ref, ...), custom_call_target="tpu_custom_call" | custom-call | flops 6442450944 | bytes 12582912 | tf_op jit(solution)/shard_map/teacher_part/pallas_call | solution.py:126
  79.7 3.0 %collective-permute-start.19 = (s16[144,1024]{1,0:T(8,128)(2,1)S(1)}, s16[144,1024]{1,0:T(8,128)(2,1)S(1)}, u32[]{:S(2)}, u32[]{:S(2)}) collective-permute-start(s16[144,1024]{1,0:T(8,128)(2,1)S(1)} %get-tuple-element.49), channel_id=1, source_target_pairs={{0,128},{64,192},{128,0},{192,64},{1,129},{65,193},{129,1},{193,65... | collective-permute-start | bytes 884744 | tf_op jit(solution)/shard_map/ppermute | solution.py:24
  83.6 2.8 %collective-permute-start.20 = (s16[144,1024]{1,0:T(8,128)(2,1)S(1)}, s16[144,1024]{1,0:T(8,128)(2,1)S(1)}, u32[]{:S(2)}, u32[]{:S(2)}) collective-permute-start(s16[144,1024]{1,0:T(8,128)(2,1)S(1)} %get-tuple-element.48), channel_id=1, source_target_pairs={{0,64},{64,128},{128,192},{192,0},{1,65},{65,129},{129,193},{193,1... | collective-permute-start | bytes 884744 | tf_op jit(solution)/shard_map/ppermute | solution.py:24
  86.4 2.7 %collective-permute-done.16 = s16[144,1024]{1,0:T(8,128)(2,1)} collective-permute-done((s16[144,1024]{1,0:T(8,128)(2,1)S(1)}, s16[144,1024]{1,0:T(8,128)(2,1)}, u32[]{:S(2)}, u32[]{:S(2)}) %collective-permute-start.16) | collective-permute-done | bytes 294944 | tf_op jit(solution)/shard_map/ppermute | solution.py:24
  97.2 19.2 %all_to_all.10 = f32[64,4,128]{2,1,0:T(4,128)S(1)} all-to-all(f32[64,4,128]{2,1,0:T(4,128)S(1)} %broadcast_in_dim.27), channel_id=1, replica_groups=mesh['y'=4,'zh'=4,'zl'=2,'xh'=2,'c'=2,'xl'=2] {'zh','zl','xh','c','xl'}, dimensions={0} | all-to-all | bytes 262144 | tf_op jit(solution)/shard_map/all_to_all | solution.py:380
  117.2 2.6 %collective-permute-start.23 = (bf16[128,1024]{1,0:T(8,128)(2,1)S(1)}, bf16[128,1024]{1,0:T(8,128)(2,1)S(1)}, u32[]{:S(2)}, u32[]{:S(2)}) collective-permute-start(bf16[128,1024]{1,0:T(8,128)(2,1)S(1)} %multiply_convert_fusion.own_ref), channel_id=1, source_target_pairs={{0,64},{64,128},{128,192},{192,0},{1,65},{65,129},{129,193},{193,1... | collective-permute-start | bytes 786440 | tf_op jit(solution)/shard_map/ppermute | solution.py:24
  119.8 5.9 %collective-permute-done.23.behind_ref = bf16[128,1024]{1,0:T(8,128)(2,1)S(1)} collective-permute-done((bf16[128,1024]{1,0:T(8,128)(2,1)S(1)}, bf16[128,1024]{1,0:T(8,128)(2,1)S(1)}, u32[]{:S(2)}, u32[]{:S(2)}) %collective-permute-start.23) | collective-permute-done | bytes 262176 | tf_op jit(solution)/shard_map/ppermute | solution.py:24
  125.7 3.8 %collective-permute-start.24 = (bf16[64,1024]{1,0:T(8,128)(2,1)S(1)}, bf16[64,1024]{1,0:T(8,128)(2,1)S(1)}, u32[]{:S(2)}, u32[]{:S(2)}) collective-permute-start(bf16[64,1024]{1,0:T(8,128)(2,1)S(1)} %slice.79), channel_id=1, source_target_pairs={{0,64},{64,128},{128,192},{192,0},{1,65},{65,129},{129,193},{193,1... | collective-permute-start | bytes 393224 | tf_op jit(solution)/shard_map/ppermute | solution.py:24
  132.0 3.8 %collective-permute-done.25.far1_ref = bf16[64,1024]{1,0:T(8,128)(2,1)S(1)} collective-permute-done((bf16[64,1024]{1,0:T(8,128)(2,1)S(1)}, bf16[64,1024]{1,0:T(8,128)(2,1)S(1)}, u32[]{:S(2)}, u32[]{:S(2)}) %collective-permute-start.25) | collective-permute-done | bytes 131104 | tf_op jit(solution)/shard_map/ppermute | solution.py:24
  141.3 2.8 %collective-permute-start.29 = (bf16[4,2,128,128]{3,2,1,0:T(8,128)(2,1)S(1)}, bf16[4,2,128,128]{3,2,1,0:T(8,128)(2,1)S(1)}, u32[]{:S(2)}, u32[]{:S(2)}) collective-permute-start(bf16[4,2,128,128]{3,2,1,0:T(8,128)(2,1)S(1)} %get-tuple-element.45), channel_id=1, source_target_pairs={{0,5},{1,0},{4,1},{5,4},{2,7},{3,2},{6,3},{7,6},{8,13},{9,8},{12,9... | collective-permute-start | bytes 786440 | tf_op jit(solution)/shard_map/ppermute | solution.py:24
  144.1 7.5 %collective-permute-done.27 = bf16[4,2,128,128]{3,2,1,0:T(8,128)(2,1)S(1)} collective-permute-done((bf16[4,2,128,128]{3,2,1,0:T(8,128)(2,1)S(1)}, bf16[4,2,128,128]{3,2,1,0:T(8,128)(2,1)S(1)}, u32[]{:S(2)}, u32[]{:S(2)}) %collective-permute-start.27) | collective-permute-done | bytes 262176 | tf_op jit(solution)/shard_map/ppermute | solution.py:24
  151.7 2.7 %collective-permute-done.29 = bf16[4,2,128,128]{3,2,1,0:T(8,128)(2,1)S(1)} collective-permute-done((bf16[4,2,128,128]{3,2,1,0:T(8,128)(2,1)S(1)}, bf16[4,2,128,128]{3,2,1,0:T(8,128)(2,1)S(1)}, u32[]{:S(2)}, u32[]{:S(2)}) %collective-permute-start.29) | collective-permute-done | bytes 262176 | tf_op jit(solution)/shard_map/ppermute | solution.py:24
  156.6 14.7 %all_to_all.11 = bf16[8,128,128]{2,1,0:T(8,128)(2,1)S(1)} all-to-all(bf16[8,128,128]{2,1,0:T(8,128)(2,1)S(1)} %bitcast.87), channel_id=1, replica_groups=mesh['y'=4,'zh'=4,'zl'=2,'xh'=2,'c'=2,'xl'=2] {'zh','zl'}, dimensions={0} | all-to-all | bytes 524288 | tf_op jit(solution)/shard_map/all_to_all | solution.py:406
  173.3 8.4 %collective-permute-done.30 = bf16[128,128]{1,0:T(8,128)(2,1)S(1)} collective-permute-done((bf16[128,128]{1,0:T(8,128)(2,1)S(1)}, bf16[128,128]{1,0:T(8,128)(2,1)S(1)}, u32[]{:S(2)}, u32[]{:S(2)}) %collective-permute-start.30) | collective-permute-done | bytes 32800 | tf_op jit(solution)/shard_map/ppermute | solution.py:408
  (109 shorter events, 37.9 us)
Async XLA Ops:
  7.2 58.7 %all-gather.2.cloned.1.call-start = ((), (), s32[]{:S(2)}) async-start(), calls=%async_computation.2 | async-start | bytes 2359296 | tf_op jit(solution)/shard_map/all_gather | solution.py:337
  7.2 8.3 %collective-permute-start.1 = (bf16[8,4096]{1,0:T(8,128)(2,1)}, bf16[8,4096]{1,0:T(8,128)(2,1)S(1)}, u32[]{:S(2)}, u32[]{:S(2)}) collective-permute-start(bf16[8,4096]{1,0:T(8,128)(2,1)} %param.9), channel_id=1, source_target_pairs={{0,4},{1,5},{4,0},{5,1},{2,6},{3,7},{6,2},{7,3},{8,12},{9,13},{12,... | collective-permute-start | bytes 196616 | tf_op jit(solution)/shard_map/ppermute | solution.py:24
  19.2 11.5 %collective-permute-start.4 = (bf16[2,128,128]{2,1,0:T(8,128)(2,1)S(1)}, bf16[2,128,128]{2,1,0:T(8,128)(2,1)S(1)}, u32[]{:S(2)}, u32[]{:S(2)}) collective-permute-start(bf16[2,128,128]{2,1,0:T(8,128)(2,1)S(1)} %pad_maximum_fusion.3), channel_id=1, source_target_pairs={{0,48},{16,112},{32,176},{48,240},{64,0},{80,64},{96,128},{112,192... | collective-permute-start | bytes 196616 | tf_op jit(solution)/shard_map/ppermute | solution.py:340
  26.1 12.8 %collective-permute-start.7 = (bf16[2,128,128]{2,1,0:T(8,128)(2,1)S(1)}, bf16[2,128,128]{2,1,0:T(8,128)(2,1)S(1)}, u32[]{:S(2)}, u32[]{:S(2)}) collective-permute-start(bf16[2,128,128]{2,1,0:T(8,128)(2,1)S(1)} %pad_maximum_fusion.3), channel_id=1, source_target_pairs={{0,0},{16,64},{32,128},{48,192},{64,16},{80,80},{96,144},{112,208}... | collective-permute-start | bytes 196616 | tf_op jit(solution)/shard_map/ppermute | solution.py:340
  30.2 8.8 %collective-permute-start.6 = (bf16[2,128,128]{2,1,0:T(8,128)(2,1)S(1)}, bf16[2,128,128]{2,1,0:T(8,128)(2,1)S(1)}, u32[]{:S(2)}, u32[]{:S(2)}) collective-permute-start(bf16[2,128,128]{2,1,0:T(8,128)(2,1)S(1)} %pad_maximum_fusion.3), channel_id=1, source_target_pairs={{0,16},{16,80},{32,144},{48,208},{64,32},{80,96},{96,160},{112,224... | collective-permute-start | bytes 196616 | tf_op jit(solution)/shard_map/ppermute | solution.py:340
  30.2 8.7 %collective-permute-start.5 = (bf16[2,128,128]{2,1,0:T(8,128)(2,1)S(1)}, bf16[2,128,128]{2,1,0:T(8,128)(2,1)S(1)}, u32[]{:S(2)}, u32[]{:S(2)}) collective-permute-start(bf16[2,128,128]{2,1,0:T(8,128)(2,1)S(1)} %pad_maximum_fusion.3), channel_id=1, source_target_pairs={{0,32},{16,96},{32,160},{48,224},{64,48},{80,112},{96,176},{112,24... | collective-permute-start | bytes 196616 | tf_op jit(solution)/shard_map/ppermute | solution.py:340
  39.1 8.2 %collective-permute-start.10 = (bf16[2,512,128]{2,1,0:T(8,128)(2,1)S(1)}, bf16[2,512,128]{2,1,0:T(8,128)(2,1)S(1)}, u32[]{:S(2)}, u32[]{:S(2)}) collective-permute-start(bf16[2,512,128]{2,1,0:T(8,128)(2,1)S(1)} %bitcast.88), channel_id=1, source_target_pairs={{0,5},{1,0},{4,1},{5,4},{2,7},{3,2},{6,3},{7,6},{8,13},{9,8},{12,9... | collective-permute-start | bytes 786440 | tf_op jit(solution)/shard_map/ppermute | solution.py:24
  42.7 10.4 %collective-permute-start.9 = (bf16[2,512,128]{2,1,0:T(8,128)(2,1)S(1)}, bf16[2,512,128]{2,1,0:T(8,128)(2,1)S(1)}, u32[]{:S(2)}, u32[]{:S(2)}) collective-permute-start(bf16[2,512,128]{2,1,0:T(8,128)(2,1)S(1)} %bitcast.89), channel_id=1, source_target_pairs={{0,1},{1,4},{4,5},{5,0},{2,3},{3,6},{6,7},{7,2},{8,9},{9,12},{12,1... | collective-permute-start | bytes 786440 | tf_op jit(solution)/shard_map/ppermute | solution.py:24
  42.7 10.4 %collective-permute-start.8 = (bf16[2,512,128]{2,1,0:T(8,128)(2,1)S(1)}, bf16[2,512,128]{2,1,0:T(8,128)(2,1)S(1)}, u32[]{:S(2)}, u32[]{:S(2)}) collective-permute-start(bf16[2,512,128]{2,1,0:T(8,128)(2,1)S(1)} %bitcast.90), channel_id=1, source_target_pairs={{0,4},{1,5},{4,0},{5,1},{2,6},{3,7},{6,2},{7,3},{8,12},{9,13},{12,... | collective-permute-start | bytes 786440 | tf_op jit(solution)/shard_map/ppermute | solution.py:24
  44.4 9.5 %collective-permute-start.11 = (bf16[2,512,128]{2,1,0:T(8,128)(2,1)S(1)}, bf16[2,512,128]{2,1,0:T(8,128)(2,1)S(1)}, u32[]{:S(2)}, u32[]{:S(2)}) collective-permute-start(bf16[2,512,128]{2,1,0:T(8,128)(2,1)S(1)} %bitcast.91), channel_id=1, source_target_pairs={{0,2},{2,0},{1,3},{3,1},{4,6},{6,4},{5,7},{7,5},{8,10},{10,8},{9,1... | collective-permute-start | bytes 786440 | tf_op jit(solution)/shard_map/ppermute | solution.py:28
  47.3 6.7 %collective-permute-start.14 = (bf16[2,512,128]{2,1,0:T(8,128)(2,1)S(1)}, bf16[2,512,128]{2,1,0:T(8,128)(2,1)S(1)}, u32[]{:S(2)}, u32[]{:S(2)}) collective-permute-start(bf16[2,512,128]{2,1,0:T(8,128)(2,1)S(1)} %collective-permute-done.10), channel_id=1, source_target_pairs={{0,2},{2,0},{1,3},{3,1},{4,6},{6,4},{5,7},{7,5},{8,10},{10,8},{9,1... | collective-permute-start | bytes 786440 | tf_op jit(solution)/shard_map/ppermute | solution.py:28
  66.5 17.1 %collective-permute-start.17 = (s16[144,1024]{1,0:T(8,128)(2,1)S(1)}, s16[144,1024]{1,0:T(8,128)(2,1)}, u32[]{:S(2)}, u32[]{:S(2)}) collective-permute-start(s16[144,1024]{1,0:T(8,128)(2,1)S(1)} %get-tuple-element.50), channel_id=1, source_target_pairs={{0,192},{64,0},{128,64},{192,128},{1,193},{65,1},{129,65},{193,129... | collective-permute-start | bytes 884744 | tf_op jit(solution)/shard_map/ppermute | solution.py:24
  67.8 21.3 %collective-permute-start.16 = (s16[144,1024]{1,0:T(8,128)(2,1)S(1)}, s16[144,1024]{1,0:T(8,128)(2,1)}, u32[]{:S(2)}, u32[]{:S(2)}) collective-permute-start(s16[144,1024]{1,0:T(8,128)(2,1)S(1)} %get-tuple-element.51), channel_id=1, source_target_pairs={{0,64},{64,128},{128,192},{192,0},{1,65},{65,129},{129,193},{193,1... | collective-permute-start | bytes 884744 | tf_op jit(solution)/shard_map/ppermute | solution.py:24
  69.8 19.3 %collective-permute-start.15 = (s16[144,1024]{1,0:T(8,128)(2,1)S(1)}, s16[144,1024]{1,0:T(8,128)(2,1)}, u32[]{:S(2)}, u32[]{:S(2)}) collective-permute-start(s16[144,1024]{1,0:T(8,128)(2,1)S(1)} %get-tuple-element.52), channel_id=1, source_target_pairs={{0,128},{64,192},{128,0},{192,64},{1,129},{65,193},{129,1},{193,65... | collective-permute-start | bytes 884744 | tf_op jit(solution)/shard_map/ppermute | solution.py:24
  79.7 11.5 %collective-permute-start.19 = (s16[144,1024]{1,0:T(8,128)(2,1)S(1)}, s16[144,1024]{1,0:T(8,128)(2,1)S(1)}, u32[]{:S(2)}, u32[]{:S(2)}) collective-permute-start(s16[144,1024]{1,0:T(8,128)(2,1)S(1)} %get-tuple-element.49), channel_id=1, source_target_pairs={{0,128},{64,192},{128,0},{192,64},{1,129},{65,193},{129,1},{193,65... | collective-permute-start | bytes 884744 | tf_op jit(solution)/shard_map/ppermute | solution.py:24
  82.9 13.7 %collective-permute-start.21 = (s16[144,1024]{1,0:T(8,128)(2,1)S(1)}, s16[144,1024]{1,0:T(8,128)(2,1)S(1)}, u32[]{:S(2)}, u32[]{:S(2)}) collective-permute-start(s16[144,1024]{1,0:T(8,128)(2,1)S(1)} %get-tuple-element.47), channel_id=1, source_target_pairs={{0,192},{64,0},{128,64},{192,128},{1,193},{65,1},{129,65},{193,129... | collective-permute-start | bytes 884744 | tf_op jit(solution)/shard_map/ppermute | solution.py:24
  83.6 13.0 %collective-permute-start.20 = (s16[144,1024]{1,0:T(8,128)(2,1)S(1)}, s16[144,1024]{1,0:T(8,128)(2,1)S(1)}, u32[]{:S(2)}, u32[]{:S(2)}) collective-permute-start(s16[144,1024]{1,0:T(8,128)(2,1)S(1)} %get-tuple-element.48), channel_id=1, source_target_pairs={{0,64},{64,128},{128,192},{192,0},{1,65},{65,129},{129,193},{193,1... | collective-permute-start | bytes 884744 | tf_op jit(solution)/shard_map/ppermute | solution.py:24
  117.2 8.5 %collective-permute-start.23 = (bf16[128,1024]{1,0:T(8,128)(2,1)S(1)}, bf16[128,1024]{1,0:T(8,128)(2,1)S(1)}, u32[]{:S(2)}, u32[]{:S(2)}) collective-permute-start(bf16[128,1024]{1,0:T(8,128)(2,1)S(1)} %multiply_convert_fusion.own_ref), channel_id=1, source_target_pairs={{0,64},{64,128},{128,192},{192,0},{1,65},{65,129},{129,193},{193,1... | collective-permute-start | bytes 786440 | tf_op jit(solution)/shard_map/ppermute | solution.py:24
  119.8 9.7 %collective-permute-start.22 = (bf16[128,1024]{1,0:T(8,128)(2,1)S(1)}, bf16[128,1024]{1,0:T(8,128)(2,1)S(1)}, u32[]{:S(2)}, u32[]{:S(2)}) collective-permute-start(bf16[128,1024]{1,0:T(8,128)(2,1)S(1)} %multiply_convert_fusion.own_ref), channel_id=1, source_target_pairs={{0,192},{64,0},{128,64},{192,128},{1,193},{65,1},{129,65},{193,129... | collective-permute-start | bytes 786440 | tf_op jit(solution)/shard_map/ppermute | solution.py:24
  125.7 6.3 %collective-permute-start.24 = (bf16[64,1024]{1,0:T(8,128)(2,1)S(1)}, bf16[64,1024]{1,0:T(8,128)(2,1)S(1)}, u32[]{:S(2)}, u32[]{:S(2)}) collective-permute-start(bf16[64,1024]{1,0:T(8,128)(2,1)S(1)} %slice.79), channel_id=1, source_target_pairs={{0,64},{64,128},{128,192},{192,0},{1,65},{65,129},{129,193},{193,1... | collective-permute-start | bytes 393224 | tf_op jit(solution)/shard_map/ppermute | solution.py:24
  140.9 10.8 %collective-permute-start.27 = (bf16[4,2,128,128]{3,2,1,0:T(8,128)(2,1)S(1)}, bf16[4,2,128,128]{3,2,1,0:T(8,128)(2,1)S(1)}, u32[]{:S(2)}, u32[]{:S(2)}) collective-permute-start(bf16[4,2,128,128]{3,2,1,0:T(8,128)(2,1)S(1)} %get-tuple-element.44), channel_id=1, source_target_pairs={{0,4},{1,5},{4,0},{5,1},{2,6},{3,7},{6,2},{7,3},{8,12},{9,13},{12,... | collective-permute-start | bytes 786440 | tf_op jit(solution)/shard_map/ppermute | solution.py:24
  141.3 13.1 %collective-permute-start.29 = (bf16[4,2,128,128]{3,2,1,0:T(8,128)(2,1)S(1)}, bf16[4,2,128,128]{3,2,1,0:T(8,128)(2,1)S(1)}, u32[]{:S(2)}, u32[]{:S(2)}) collective-permute-start(bf16[4,2,128,128]{3,2,1,0:T(8,128)(2,1)S(1)} %get-tuple-element.45), channel_id=1, source_target_pairs={{0,5},{1,0},{4,1},{5,4},{2,7},{3,2},{6,3},{7,6},{8,13},{9,8},{12,9... | collective-permute-start | bytes 786440 | tf_op jit(solution)/shard_map/ppermute | solution.py:24
  144.1 12.3 %collective-permute-start.28 = (bf16[4,2,128,128]{3,2,1,0:T(8,128)(2,1)S(1)}, bf16[4,2,128,128]{3,2,1,0:T(8,128)(2,1)S(1)}, u32[]{:S(2)}, u32[]{:S(2)}) collective-permute-start(bf16[4,2,128,128]{3,2,1,0:T(8,128)(2,1)S(1)} %get-tuple-element.46), channel_id=1, source_target_pairs={{0,1},{1,4},{4,5},{5,0},{2,3},{3,6},{6,7},{7,2},{8,9},{9,12},{12,1... | collective-permute-start | bytes 786440 | tf_op jit(solution)/shard_map/ppermute | solution.py:24
  171.4 10.4 %collective-permute-start.30 = (bf16[128,128]{1,0:T(8,128)(2,1)S(1)}, bf16[128,128]{1,0:T(8,128)(2,1)S(1)}, u32[]{:S(2)}, u32[]{:S(2)}) collective-permute-start(bf16[128,128]{1,0:T(8,128)(2,1)S(1)} %reduce_sum.52), channel_id=1, source_target_pairs={{0,0},{16,64},{32,128},{48,192},{64,16},{80,80},{96,144},{112,208}... | collective-permute-start | bytes 98312 | tf_op jit(solution)/shard_map/ppermute | solution.py:408
  (12 other events, 96.2 us)
Sparse Core Ops, SparseCore 0:
  17.8 48.0 all-gather.1

commit v4 on v3

--- a/solution.py
+++ b/solution.py
@@ -392,10 +392,10 @@
     half = tok_rows // 2
     delta, student_head = lax.optimization_barrier((delta, student_head))
     student_head = bring(student_head)
+    far = shift(delta, "y", NY, 2)
     behind = shift(delta, "y", NY, 1)
     front = shift(delta, "y", NY, -1)
-    far = [shift(behind[:half], "y", NY, 1), shift(front[half:], "y", NY, -1)]
-    pieces = [delta, front] + far + [behind]
+    pieces = [delta, front, far[:half], far[half:], behind]
 
     theirs = other_core(gradient_part(1 - c, x, y, pieces, student_head, bf16))
     mine = gradient_part(c, x, y, pieces, student_head, f32)

time: 190 us -> 189 us (level); the launches traced: 189 us -> 186 us
  waiting for transfers between devices: 62.4 us -> 58.9 us
    ppermute x1, waiting for transfers between devices: 8.45 us -> 5.81 us  [per_device(): hidden_grad = lax.ppermute(grad, ('y', 'zh'), swap_pairs(0))]
    ppermute x1, starting transfers between devices: 1.92 us -> 4.21 us  [per_device(): hidden_grad = lax.ppermute(grad, ('y', 'zh'), swap_pairs(0))]
    ppermute x19 -> x18, starting transfers between devices: 30.9 us -> 28.8 us  [shift(): return lax.ppermute(a, axes, [(i, (i + k) % n) for i in range(n)])]
    ppermute x19 -> x18, waiting for transfers between devices: 38.2 us -> 37.3 us  [shift(): return lax.ppermute(a, axes, [(i, (i + k) % n) for i in range(n)])]
  transfers between devices with their start and end apart: 32 -> 31, of which waited for: 21 -> 21; matrix products, arithmetic and copies ran while one was open for 4% -> 5% of each run, Pallas kernels for 10% -> 10%
where the time goes in v4:
time: 189 us; the launch traced here: 186 us
  waiting for transfers between devices  58.9 us (31%)
  starting transfers between devices  47 us (25%)
  blocking collectives  33.9 us (18%)
  Pallas kernels  21.1 us (11%)
  between operations  14.4 us (8%)
  other arithmetic  9.21 us (5%)
    ppermute x18, waiting for transfers between devices, shift(): return lax.ppermute(a, axes, [(i, (i + k) % n) for i in range(n)])  37.3 us
    ppermute x18, starting transfers between devices, shift(): return lax.ppermute(a, axes, [(i, (i + k) % n) for i in range(n)])  28.8 us
    all_to_all x1, blocking collectives, per_device(): lax.all_to_all(jnp.broadcast_to(sums[None], (64,) + sums.shape), VOCAB, 0...  19.2 us
    all_to_all x1, blocking collectives, per_device(): lax.all_to_all(grad.astype(bf16).reshape(NZ, tok_rows, feats), Z, 0, 0)  14.7 us
    ppermute x4, starting transfers between devices, per_device(): lax.ppermute(got, ('y', 'zh'), swap_pairs(k))  11.4 us
    pallas_call x1, Pallas kernels, teacher_part(): pl.pallas_call(teacher_kernel, in_specs=in_vmem(2) + in_hbm(3), out_specs...  9.17 us
    ppermute x4, waiting for transfers between devices, per_device(): lax.ppermute(got, ('y', 'zh'), swap_pairs(k))  8.2 us
    ppermute x1, waiting for transfers between devices, per_device(): hidden_grad = lax.ppermute(grad, ('y', 'zh'), swap_pairs(0))  5.81 us
  transfers between devices with their start and end apart: 31, of which 21 were waited for; matrix products, arithmetic and copies ran while one was open for 5% of the time, Pallas kernels for 10%

profile of v4, /device:TPU:24, one launch (start us, length us, event | category | flops | bytes accessed | tf_op | source)
XLA Modules:
  0.0 185.9 jit_solution(7063036135269341957)
XLA Ops:
  7.2 3.1 %collective-permute-start.1 = (bf16[8,4096]{1,0:T(8,128)(2,1)}, bf16[8,4096]{1,0:T(8,128)(2,1)S(1)}, u32[]{:S(2)}, u32[]{:S(2)}) collective-permute-start(bf16[8,4096]{1,0:T(8,128)(2,1)} %param.9), channel_id=1, source_target_pairs={{0,4},{1,5},{4,0},{5,1},{2,6},{3,7},{6,2},{7,3},{8,12},{9,13},{12,... | collective-permute-start | bytes 196616 | tf_op jit(solution)/shard_map/ppermute | solution.py:24
  10.9 2.6 %collective-permute-start.2 = (bf16[8,4096]{1,0:T(8,128)(2,1)}, bf16[8,4096]{1,0:T(8,128)(2,1)S(1)}, u32[]{:S(2)}, u32[]{:S(2)}) collective-permute-start(bf16[8,4096]{1,0:T(8,128)(2,1)} %param.9), channel_id=1, source_target_pairs={{0,5},{1,0},{4,1},{5,4},{2,7},{3,2},{6,3},{7,6},{8,13},{9,8},{12,9... | collective-permute-start | bytes 196616 | tf_op jit(solution)/shard_map/ppermute | solution.py:24
  19.2 6.8 %collective-permute-start.4 = (bf16[2,128,128]{2,1,0:T(8,128)(2,1)S(1)}, bf16[2,128,128]{2,1,0:T(8,128)(2,1)S(1)}, u32[]{:S(2)}, u32[]{:S(2)}) collective-permute-start(bf16[2,128,128]{2,1,0:T(8,128)(2,1)S(1)} %pad_maximum_fusion.3), channel_id=1, source_target_pairs={{0,48},{16,112},{32,176},{48,240},{64,0},{80,64},{96,128},{112,192... | collective-permute-start | bytes 196616 | tf_op jit(solution)/shard_map/ppermute | solution.py:340
  26.1 4.0 %collective-permute-start.7 = (bf16[2,128,128]{2,1,0:T(8,128)(2,1)S(1)}, bf16[2,128,128]{2,1,0:T(8,128)(2,1)S(1)}, u32[]{:S(2)}, u32[]{:S(2)}) collective-permute-start(bf16[2,128,128]{2,1,0:T(8,128)(2,1)S(1)} %pad_maximum_fusion.3), channel_id=1, source_target_pairs={{0,0},{16,64},{32,128},{48,192},{64,16},{80,80},{96,144},{112,208}... | collective-permute-start | bytes 196616 | tf_op jit(solution)/shard_map/ppermute | solution.py:340
  30.7 8.2 %collective-permute-done.5 = bf16[2,128,128]{2,1,0:T(8,128)(2,1)S(1)} collective-permute-done((bf16[2,128,128]{2,1,0:T(8,128)(2,1)S(1)}, bf16[2,128,128]{2,1,0:T(8,128)(2,1)S(1)}, u32[]{:S(2)}, u32[]{:S(2)}) %collective-permute-start.5) | collective-permute-done | bytes 65568 | tf_op jit(solution)/shard_map/ppermute | solution.py:340
  39.1 3.6 %collective-permute-start.10 = (bf16[2,512,128]{2,1,0:T(8,128)(2,1)S(1)}, bf16[2,512,128]{2,1,0:T(8,128)(2,1)S(1)}, u32[]{:S(2)}, u32[]{:S(2)}) collective-permute-start(bf16[2,512,128]{2,1,0:T(8,128)(2,1)S(1)} %bitcast.88), channel_id=1, source_target_pairs={{0,5},{1,0},{4,1},{5,4},{2,7},{3,2},{6,3},{7,6},{8,13},{9,8},{12,9... | collective-permute-start | bytes 786440 | tf_op jit(solution)/shard_map/ppermute | solution.py:24
  44.4 2.8 %collective-permute-done.10 = bf16[2,512,128]{2,1,0:T(8,128)(2,1)S(1)} collective-permute-done((bf16[2,512,128]{2,1,0:T(8,128)(2,1)S(1)}, bf16[2,512,128]{2,1,0:T(8,128)(2,1)S(1)}, u32[]{:S(2)}, u32[]{:S(2)}) %collective-permute-start.10) | collective-permute-done | bytes 262176 | tf_op jit(solution)/shard_map/ppermute | solution.py:24
  47.3 5.8 %collective-permute-done.9 = bf16[2,512,128]{2,1,0:T(8,128)(2,1)S(1)} collective-permute-done((bf16[2,512,128]{2,1,0:T(8,128)(2,1)S(1)}, bf16[2,512,128]{2,1,0:T(8,128)(2,1)S(1)}, u32[]{:S(2)}, u32[]{:S(2)}) %collective-permute-start.9) | collective-permute-done | bytes 262176 | tf_op jit(solution)/shard_map/ppermute | solution.py:24
  55.2 5.4 %student_part.1 = (s16[3,144,1024]{2,1,0:T(8,128)(2,1)S(1)}, f32[128,1024]{1,0:T(8,128)S(1)}) custom-call(s32[16]{0:T(128)S(1)} %add.248.order_ref, bf16[8,512,128]{2,1,0:T(8,128)(2,1)S(1)} %pad_maximum_fusion.mine_ref, bf16[8,512,128]{2,1,0:T(8,128)(2,1)S(1)} %pad_maximum_fusion.1.other_ref, bf16[2048,1024]{1,0:T(8,128)(2,1)} %head_ref.4), custom_call_target="tpu_custom_call" | custom-call | flops 2147483648 | bytes 6291456 | tf_op jit(solution)/shard_map/student_part/pallas_call | solution.py:170
  60.6 5.3 %all-gather.2.cloned.1.call-done.mine_ref = bf16[256,4096]{1,0:T(8,128)(2,1)} async-done(((bf16[32,4096]{1,0:T(8,128)(2,1)}), bf16[256,4096]{1,0:T(8,128)(2,1)}) %all-gather.2.cloned.1.call-update) | async-done | bytes 2097168 | tf_op jit(solution)/shard_map/all_gather | solution.py:337
  70.4 9.2 %teacher_part.1 = (s16[3,144,1024]{2,1,0:T(8,128)(2,1)S(1)}, f32[128,1024]{1,0:T(8,128)S(1)}) custom-call(s32[512,1]{1,0:T(8,128)S(1)} %copy.18.ahead_ref, s32[1,512]{1,0:T(1,128)S(1)} %add.265.places_ref, bf16[256,4096]{1,0:T(8,128)(2,1)} %all-gather.2.cloned.1.call-done.mine_ref, bf16[256,4096]{1,0:T(8,128)(2,1)} %collective-permute-done.18.other_ref, ...), custom_call_target="tpu_custom_call" | custom-call | flops 6442450944 | bytes 12582912 | tf_op jit(solution)/shard_map/teacher_part/pallas_call | solution.py:126
  79.7 3.0 %collective-permute-start.19 = (s16[144,1024]{1,0:T(8,128)(2,1)S(1)}, s16[144,1024]{1,0:T(8,128)(2,1)S(1)}, u32[]{:S(2)}, u32[]{:S(2)}) collective-permute-start(s16[144,1024]{1,0:T(8,128)(2,1)S(1)} %get-tuple-element.49), channel_id=1, source_target_pairs={{0,128},{64,192},{128,0},{192,64},{1,129},{65,193},{129,1},{193,65... | collective-permute-start | bytes 884744 | tf_op jit(solution)/shard_map/ppermute | solution.py:24
  83.6 2.8 %collective-permute-start.20 = (s16[144,1024]{1,0:T(8,128)(2,1)S(1)}, s16[144,1024]{1,0:T(8,128)(2,1)S(1)}, u32[]{:S(2)}, u32[]{:S(2)}) collective-permute-start(s16[144,1024]{1,0:T(8,128)(2,1)S(1)} %get-tuple-element.48), channel_id=1, source_target_pairs={{0,64},{64,128},{128,192},{192,0},{1,65},{65,129},{129,193},{193,1... | collective-permute-start | bytes 884744 | tf_op jit(solution)/shard_map/ppermute | solution.py:24
  86.4 2.7 %collective-permute-done.16 = s16[144,1024]{1,0:T(8,128)(2,1)} collective-permute-done((s16[144,1024]{1,0:T(8,128)(2,1)S(1)}, s16[144,1024]{1,0:T(8,128)(2,1)}, u32[]{:S(2)}, u32[]{:S(2)}) %collective-permute-start.16) | collective-permute-done | bytes 294944 | tf_op jit(solution)/shard_map/ppermute | solution.py:24
  97.2 19.2 %all_to_all.10 = f32[64,4,128]{2,1,0:T(4,128)S(1)} all-to-all(f32[64,4,128]{2,1,0:T(4,128)S(1)} %broadcast_in_dim.27), channel_id=1, replica_groups=mesh['y'=4,'zh'=4,'zl'=2,'xh'=2,'c'=2,'xl'=2] {'zh','zl','xh','c','xl'}, dimensions={0} | all-to-all | bytes 262144 | tf_op jit(solution)/shard_map/all_to_all | solution.py:380
  117.2 2.3 %collective-permute-start.23 = (bf16[128,1024]{1,0:T(8,128)(2,1)S(1)}, bf16[128,1024]{1,0:T(8,128)(2,1)S(1)}, u32[]{:S(2)}, u32[]{:S(2)}) collective-permute-start(bf16[128,1024]{1,0:T(8,128)(2,1)S(1)} %multiply_convert_fusion.own_ref), channel_id=1, source_target_pairs={{0,128},{64,192},{128,0},{192,64},{1,129},{65,193},{129,1},{193,65... | collective-permute-start | bytes 786440 | tf_op jit(solution)/shard_map/ppermute | solution.py:24
  123.9 4.2 %collective-permute-done.23 = bf16[128,1024]{1,0:T(8,128)(2,1)S(1)} collective-permute-done((bf16[128,1024]{1,0:T(8,128)(2,1)S(1)}, bf16[128,1024]{1,0:T(8,128)(2,1)S(1)}, u32[]{:S(2)}, u32[]{:S(2)}) %collective-permute-start.23) | collective-permute-done | bytes 262176 | tf_op jit(solution)/shard_map/ppermute | solution.py:24
  128.1 4.6 %collective-permute-done.24.behind_ref = bf16[128,1024]{1,0:T(8,128)(2,1)S(1)} collective-permute-done((bf16[128,1024]{1,0:T(8,128)(2,1)S(1)}, bf16[128,1024]{1,0:T(8,128)(2,1)S(1)}, u32[]{:S(2)}, u32[]{:S(2)}) %collective-permute-start.24) | collective-permute-done | bytes 262176 | tf_op jit(solution)/shard_map/ppermute | solution.py:24
  138.4 2.8 %collective-permute-start.28 = (bf16[4,2,128,128]{3,2,1,0:T(8,128)(2,1)S(1)}, bf16[4,2,128,128]{3,2,1,0:T(8,128)(2,1)S(1)}, u32[]{:S(2)}, u32[]{:S(2)}) collective-permute-start(bf16[4,2,128,128]{3,2,1,0:T(8,128)(2,1)S(1)} %get-tuple-element.45), channel_id=1, source_target_pairs={{0,5},{1,0},{4,1},{5,4},{2,7},{3,2},{6,3},{7,6},{8,13},{9,8},{12,9... | collective-permute-start | bytes 786440 | tf_op jit(solution)/shard_map/ppermute | solution.py:24
  141.2 7.5 %collective-permute-done.26 = bf16[4,2,128,128]{3,2,1,0:T(8,128)(2,1)S(1)} collective-permute-done((bf16[4,2,128,128]{3,2,1,0:T(8,128)(2,1)S(1)}, bf16[4,2,128,128]{3,2,1,0:T(8,128)(2,1)S(1)}, u32[]{:S(2)}, u32[]{:S(2)}) %collective-permute-start.26) | collective-permute-done | bytes 262176 | tf_op jit(solution)/shard_map/ppermute | solution.py:24
  148.7 2.7 %collective-permute-done.28 = bf16[4,2,128,128]{3,2,1,0:T(8,128)(2,1)S(1)} collective-permute-done((bf16[4,2,128,128]{3,2,1,0:T(8,128)(2,1)S(1)}, bf16[4,2,128,128]{3,2,1,0:T(8,128)(2,1)S(1)}, u32[]{:S(2)}, u32[]{:S(2)}) %collective-permute-start.28) | collective-permute-done | bytes 262176 | tf_op jit(solution)/shard_map/ppermute | solution.py:24
  153.6 14.7 %all_to_all.11 = bf16[8,128,128]{2,1,0:T(8,128)(2,1)S(1)} all-to-all(bf16[8,128,128]{2,1,0:T(8,128)(2,1)S(1)} %bitcast.87), channel_id=1, replica_groups=mesh['y'=4,'zh'=4,'zl'=2,'xh'=2,'c'=2,'xl'=2] {'zh','zl'}, dimensions={0} | all-to-all | bytes 524288 | tf_op jit(solution)/shard_map/all_to_all | solution.py:406
  168.4 4.2 %collective-permute-start.29 = (bf16[128,128]{1,0:T(8,128)(2,1)S(1)}, bf16[128,128]{1,0:T(8,128)(2,1)S(1)}, u32[]{:S(2)}, u32[]{:S(2)}) collective-permute-start(bf16[128,128]{1,0:T(8,128)(2,1)S(1)} %reduce_sum.52), channel_id=1, source_target_pairs={{0,0},{16,64},{32,128},{48,192},{64,16},{80,80},{96,144},{112,208}... | collective-permute-start | bytes 98312 | tf_op jit(solution)/shard_map/ppermute | solution.py:408
  172.6 5.8 %collective-permute-done.29 = bf16[128,128]{1,0:T(8,128)(2,1)S(1)} collective-permute-done((bf16[128,128]{1,0:T(8,128)(2,1)S(1)}, bf16[128,128]{1,0:T(8,128)(2,1)S(1)}, u32[]{:S(2)}, u32[]{:S(2)}) %collective-permute-start.29) | collective-permute-done | bytes 32800 | tf_op jit(solution)/shard_map/ppermute | solution.py:408
  (106 shorter events, 37.9 us)
Async XLA Ops:
  7.2 58.7 %all-gather.2.cloned.1.call-start = ((), (), s32[]{:S(2)}) async-start(), calls=%async_computation.2 | async-start | bytes 2359296 | tf_op jit(solution)/shard_map/all_gather | solution.py:337
  7.2 8.3 %collective-permute-start.1 = (bf16[8,4096]{1,0:T(8,128)(2,1)}, bf16[8,4096]{1,0:T(8,128)(2,1)S(1)}, u32[]{:S(2)}, u32[]{:S(2)}) collective-permute-start(bf16[8,4096]{1,0:T(8,128)(2,1)} %param.9), channel_id=1, source_target_pairs={{0,4},{1,5},{4,0},{5,1},{2,6},{3,7},{6,2},{7,3},{8,12},{9,13},{12,... | collective-permute-start | bytes 196616 | tf_op jit(solution)/shard_map/ppermute | solution.py:24
  19.2 11.5 %collective-permute-start.4 = (bf16[2,128,128]{2,1,0:T(8,128)(2,1)S(1)}, bf16[2,128,128]{2,1,0:T(8,128)(2,1)S(1)}, u32[]{:S(2)}, u32[]{:S(2)}) collective-permute-start(bf16[2,128,128]{2,1,0:T(8,128)(2,1)S(1)} %pad_maximum_fusion.3), channel_id=1, source_target_pairs={{0,48},{16,112},{32,176},{48,240},{64,0},{80,64},{96,128},{112,192... | collective-permute-start | bytes 196616 | tf_op jit(solution)/shard_map/ppermute | solution.py:340
  26.1 12.8 %collective-permute-start.7 = (bf16[2,128,128]{2,1,0:T(8,128)(2,1)S(1)}, bf16[2,128,128]{2,1,0:T(8,128)(2,1)S(1)}, u32[]{:S(2)}, u32[]{:S(2)}) collective-permute-start(bf16[2,128,128]{2,1,0:T(8,128)(2,1)S(1)} %pad_maximum_fusion.3), channel_id=1, source_target_pairs={{0,0},{16,64},{32,128},{48,192},{64,16},{80,80},{96,144},{112,208}... | collective-permute-start | bytes 196616 | tf_op jit(solution)/shard_map/ppermute | solution.py:340
  30.2 8.8 %collective-permute-start.6 = (bf16[2,128,128]{2,1,0:T(8,128)(2,1)S(1)}, bf16[2,128,128]{2,1,0:T(8,128)(2,1)S(1)}, u32[]{:S(2)}, u32[]{:S(2)}) collective-permute-start(bf16[2,128,128]{2,1,0:T(8,128)(2,1)S(1)} %pad_maximum_fusion.3), channel_id=1, source_target_pairs={{0,16},{16,80},{32,144},{48,208},{64,32},{80,96},{96,160},{112,224... | collective-permute-start | bytes 196616 | tf_op jit(solution)/shard_map/ppermute | solution.py:340
  30.2 8.7 %collective-permute-start.5 = (bf16[2,128,128]{2,1,0:T(8,128)(2,1)S(1)}, bf16[2,128,128]{2,1,0:T(8,128)(2,1)S(1)}, u32[]{:S(2)}, u32[]{:S(2)}) collective-permute-start(bf16[2,128,128]{2,1,0:T(8,128)(2,1)S(1)} %pad_maximum_fusion.3), channel_id=1, source_target_pairs={{0,32},{16,96},{32,160},{48,224},{64,48},{80,112},{96,176},{112,24... | collective-permute-start | bytes 196616 | tf_op jit(solution)/shard_map/ppermute | solution.py:340
  39.1 8.2 %collective-permute-start.10 = (bf16[2,512,128]{2,1,0:T(8,128)(2,1)S(1)}, bf16[2,512,128]{2,1,0:T(8,128)(2,1)S(1)}, u32[]{:S(2)}, u32[]{:S(2)}) collective-permute-start(bf16[2,512,128]{2,1,0:T(8,128)(2,1)S(1)} %bitcast.88), channel_id=1, source_target_pairs={{0,5},{1,0},{4,1},{5,4},{2,7},{3,2},{6,3},{7,6},{8,13},{9,8},{12,9... | collective-permute-start | bytes 786440 | tf_op jit(solution)/shard_map/ppermute | solution.py:24
  42.7 10.4 %collective-permute-start.9 = (bf16[2,512,128]{2,1,0:T(8,128)(2,1)S(1)}, bf16[2,512,128]{2,1,0:T(8,128)(2,1)S(1)}, u32[]{:S(2)}, u32[]{:S(2)}) collective-permute-start(bf16[2,512,128]{2,1,0:T(8,128)(2,1)S(1)} %bitcast.89), channel_id=1, source_target_pairs={{0,1},{1,4},{4,5},{5,0},{2,3},{3,6},{6,7},{7,2},{8,9},{9,12},{12,1... | collective-permute-start | bytes 786440 | tf_op jit(solution)/shard_map/ppermute | solution.py:24
  42.7 10.4 %collective-permute-start.8 = (bf16[2,512,128]{2,1,0:T(8,128)(2,1)S(1)}, bf16[2,512,128]{2,1,0:T(8,128)(2,1)S(1)}, u32[]{:S(2)}, u32[]{:S(2)}) collective-permute-start(bf16[2,512,128]{2,1,0:T(8,128)(2,1)S(1)} %bitcast.90), channel_id=1, source_target_pairs={{0,4},{1,5},{4,0},{5,1},{2,6},{3,7},{6,2},{7,3},{8,12},{9,13},{12,... | collective-permute-start | bytes 786440 | tf_op jit(solution)/shard_map/ppermute | solution.py:24
  44.4 9.5 %collective-permute-start.11 = (bf16[2,512,128]{2,1,0:T(8,128)(2,1)S(1)}, bf16[2,512,128]{2,1,0:T(8,128)(2,1)S(1)}, u32[]{:S(2)}, u32[]{:S(2)}) collective-permute-start(bf16[2,512,128]{2,1,0:T(8,128)(2,1)S(1)} %bitcast.91), channel_id=1, source_target_pairs={{0,2},{2,0},{1,3},{3,1},{4,6},{6,4},{5,7},{7,5},{8,10},{10,8},{9,1... | collective-permute-start | bytes 786440 | tf_op jit(solution)/shard_map/ppermute | solution.py:28
  47.3 6.7 %collective-permute-start.14 = (bf16[2,512,128]{2,1,0:T(8,128)(2,1)S(1)}, bf16[2,512,128]{2,1,0:T(8,128)(2,1)S(1)}, u32[]{:S(2)}, u32[]{:S(2)}) collective-permute-start(bf16[2,512,128]{2,1,0:T(8,128)(2,1)S(1)} %collective-permute-done.10), channel_id=1, source_target_pairs={{0,2},{2,0},{1,3},{3,1},{4,6},{6,4},{5,7},{7,5},{8,10},{10,8},{9,1... | collective-permute-start | bytes 786440 | tf_op jit(solution)/shard_map/ppermute | solution.py:28
  66.5 17.1 %collective-permute-start.17 = (s16[144,1024]{1,0:T(8,128)(2,1)S(1)}, s16[144,1024]{1,0:T(8,128)(2,1)}, u32[]{:S(2)}, u32[]{:S(2)}) collective-permute-start(s16[144,1024]{1,0:T(8,128)(2,1)S(1)} %get-tuple-element.50), channel_id=1, source_target_pairs={{0,192},{64,0},{128,64},{192,128},{1,193},{65,1},{129,65},{193,129... | collective-permute-start | bytes 884744 | tf_op jit(solution)/shard_map/ppermute | solution.py:24
  67.8 21.3 %collective-permute-start.16 = (s16[144,1024]{1,0:T(8,128)(2,1)S(1)}, s16[144,1024]{1,0:T(8,128)(2,1)}, u32[]{:S(2)}, u32[]{:S(2)}) collective-permute-start(s16[144,1024]{1,0:T(8,128)(2,1)S(1)} %get-tuple-element.51), channel_id=1, source_target_pairs={{0,64},{64,128},{128,192},{192,0},{1,65},{65,129},{129,193},{193,1... | collective-permute-start | bytes 884744 | tf_op jit(solution)/shard_map/ppermute | solution.py:24
  69.8 19.3 %collective-permute-start.15 = (s16[144,1024]{1,0:T(8,128)(2,1)S(1)}, s16[144,1024]{1,0:T(8,128)(2,1)}, u32[]{:S(2)}, u32[]{:S(2)}) collective-permute-start(s16[144,1024]{1,0:T(8,128)(2,1)S(1)} %get-tuple-element.52), channel_id=1, source_target_pairs={{0,128},{64,192},{128,0},{192,64},{1,129},{65,193},{129,1},{193,65... | collective-permute-start | bytes 884744 | tf_op jit(solution)/shard_map/ppermute | solution.py:24
  79.7 11.5 %collective-permute-start.19 = (s16[144,1024]{1,0:T(8,128)(2,1)S(1)}, s16[144,1024]{1,0:T(8,128)(2,1)S(1)}, u32[]{:S(2)}, u32[]{:S(2)}) collective-permute-start(s16[144,1024]{1,0:T(8,128)(2,1)S(1)} %get-tuple-element.49), channel_id=1, source_target_pairs={{0,128},{64,192},{128,0},{192,64},{1,129},{65,193},{129,1},{193,65... | collective-permute-start | bytes 884744 | tf_op jit(solution)/shard_map/ppermute | solution.py:24
  82.9 13.7 %collective-permute-start.21 = (s16[144,1024]{1,0:T(8,128)(2,1)S(1)}, s16[144,1024]{1,0:T(8,128)(2,1)S(1)}, u32[]{:S(2)}, u32[]{:S(2)}) collective-permute-start(s16[144,1024]{1,0:T(8,128)(2,1)S(1)} %get-tuple-element.47), channel_id=1, source_target_pairs={{0,192},{64,0},{128,64},{192,128},{1,193},{65,1},{129,65},{193,129... | collective-permute-start | bytes 884744 | tf_op jit(solution)/shard_map/ppermute | solution.py:24
  83.6 13.0 %collective-permute-start.20 = (s16[144,1024]{1,0:T(8,128)(2,1)S(1)}, s16[144,1024]{1,0:T(8,128)(2,1)S(1)}, u32[]{:S(2)}, u32[]{:S(2)}) collective-permute-start(s16[144,1024]{1,0:T(8,128)(2,1)S(1)} %get-tuple-element.48), channel_id=1, source_target_pairs={{0,64},{64,128},{128,192},{192,0},{1,65},{65,129},{129,193},{193,1... | collective-permute-start | bytes 884744 | tf_op jit(solution)/shard_map/ppermute | solution.py:24
  117.2 10.8 %collective-permute-start.23 = (bf16[128,1024]{1,0:T(8,128)(2,1)S(1)}, bf16[128,1024]{1,0:T(8,128)(2,1)S(1)}, u32[]{:S(2)}, u32[]{:S(2)}) collective-permute-start(bf16[128,1024]{1,0:T(8,128)(2,1)S(1)} %multiply_convert_fusion.own_ref), channel_id=1, source_target_pairs={{0,128},{64,192},{128,0},{192,64},{1,129},{65,193},{129,1},{193,65... | collective-permute-start | bytes 786440 | tf_op jit(solution)/shard_map/ppermute | solution.py:24
  119.6 13.1 %collective-permute-start.24 = (bf16[128,1024]{1,0:T(8,128)(2,1)S(1)}, bf16[128,1024]{1,0:T(8,128)(2,1)S(1)}, u32[]{:S(2)}, u32[]{:S(2)}) collective-permute-start(bf16[128,1024]{1,0:T(8,128)(2,1)S(1)} %multiply_convert_fusion.own_ref), channel_id=1, source_target_pairs={{0,64},{64,128},{128,192},{192,0},{1,65},{65,129},{129,193},{193,1... | collective-permute-start | bytes 786440 | tf_op jit(solution)/shard_map/ppermute | solution.py:24
  121.0 11.8 %collective-permute-start.22 = (bf16[128,1024]{1,0:T(8,128)(2,1)S(1)}, bf16[128,1024]{1,0:T(8,128)(2,1)S(1)}, u32[]{:S(2)}, u32[]{:S(2)}) collective-permute-start(bf16[128,1024]{1,0:T(8,128)(2,1)S(1)} %multiply_convert_fusion.own_ref), channel_id=1, source_target_pairs={{0,192},{64,0},{128,64},{192,128},{1,193},{65,1},{129,65},{193,129... | collective-permute-start | bytes 786440 | tf_op jit(solution)/shard_map/ppermute | solution.py:24
  137.9 10.8 %collective-permute-start.26 = (bf16[4,2,128,128]{3,2,1,0:T(8,128)(2,1)S(1)}, bf16[4,2,128,128]{3,2,1,0:T(8,128)(2,1)S(1)}, u32[]{:S(2)}, u32[]{:S(2)}) collective-permute-start(bf16[4,2,128,128]{3,2,1,0:T(8,128)(2,1)S(1)} %get-tuple-element.44), channel_id=1, source_target_pairs={{0,4},{1,5},{4,0},{5,1},{2,6},{3,7},{6,2},{7,3},{8,12},{9,13},{12,... | collective-permute-start | bytes 786440 | tf_op jit(solution)/shard_map/ppermute | solution.py:24
  138.4 13.1 %collective-permute-start.28 = (bf16[4,2,128,128]{3,2,1,0:T(8,128)(2,1)S(1)}, bf16[4,2,128,128]{3,2,1,0:T(8,128)(2,1)S(1)}, u32[]{:S(2)}, u32[]{:S(2)}) collective-permute-start(bf16[4,2,128,128]{3,2,1,0:T(8,128)(2,1)S(1)} %get-tuple-element.45), channel_id=1, source_target_pairs={{0,5},{1,0},{4,1},{5,4},{2,7},{3,2},{6,3},{7,6},{8,13},{9,8},{12,9... | collective-permute-start | bytes 786440 | tf_op jit(solution)/shard_map/ppermute | solution.py:24
  141.2 12.3 %collective-permute-start.27 = (bf16[4,2,128,128]{3,2,1,0:T(8,128)(2,1)S(1)}, bf16[4,2,128,128]{3,2,1,0:T(8,128)(2,1)S(1)}, u32[]{:S(2)}, u32[]{:S(2)}) collective-permute-start(bf16[4,2,128,128]{3,2,1,0:T(8,128)(2,1)S(1)} %get-tuple-element.46), channel_id=1, source_target_pairs={{0,1},{1,4},{4,5},{5,0},{2,3},{3,6},{6,7},{7,2},{8,9},{9,12},{12,1... | collective-permute-start | bytes 786440 | tf_op jit(solution)/shard_map/ppermute | solution.py:24
  168.4 10.0 %collective-permute-start.29 = (bf16[128,128]{1,0:T(8,128)(2,1)S(1)}, bf16[128,128]{1,0:T(8,128)(2,1)S(1)}, u32[]{:S(2)}, u32[]{:S(2)}) collective-permute-start(bf16[128,128]{1,0:T(8,128)(2,1)S(1)} %reduce_sum.52), channel_id=1, source_target_pairs={{0,0},{16,64},{32,128},{48,192},{64,16},{80,80},{96,144},{112,208}... | collective-permute-start | bytes 98312 | tf_op jit(solution)/shard_map/ppermute | solution.py:408
  (11 other events, 89.9 us)
Sparse Core Ops, SparseCore 0:
  17.8 48.0 all-gather.1
